TPU v7x, 128 devices: a whole 4x4x4 slice. The times are simulated.
128 devices in a mesh: row: 8 (over y_lo, x), col: 16 (over y_hi, z, core).
Axes of the slice: x: 4, y: 4 (y_hi: 2, y_lo: 2; y = y_hi * 2 + y_lo), z: 4, core: 2. Of those that a mesh axis runs over, the one named last changes fastest.
Arguments:
- pair_rep: bfloat16 [512, 512, 128], P('row', 'col'), may hold values from -40 to 40
- residue_mask: int32 [512], replicated, may hold values 0 or 1
- chain_index: int32 [512], replicated, may hold values from 0 to 5, never falling along the last dimension, each value on 1 to 256 neighbouring positions
- mul_in: bfloat16 [128, 512], replicated, may hold values from -0.5 to 0.5
- mul_gate: bfloat16 [128, 128], replicated, may hold values from -0.5 to 0.5
- mul_out: bfloat16 [128, 128], replicated, may hold values from -0.5 to 0.5
- att_in: bfloat16 [128, 512], replicated, may hold values from -0.5 to 0.5
- att_bias: bfloat16 [128, 4], replicated, may hold values from -28 to 28
- chain_bias: float32 [4], replicated, may hold values from -5 to 5
- att_out: bfloat16 [128, 128], replicated, may hold values from -0.5 to 0.5
- trans_up: bfloat16 [128, 512], replicated, may hold values from -0.5 to 0.5
- trans_down: bfloat16 [512, 128], replicated, may hold values from -0.25 to 0.25
Outputs:
- new_pair: bfloat16 [512, 512, 128], P('row', 'col')
All inputs are finite; a program needn't handle non-finite values.
Results may differ from a plain program's by a relative error of at most 0.04.
The roundings to bfloat16 on the way count: a program that leaves them out, or rounds other values in their place, can miss the bound.
Values may be sent and summed in bfloat16 or wider, within the bound.
A program may use at most 128 MiB of HBM per device.

v0:
```python
import math

import jax
import jax.numpy as jnp
from jax import lax
from jax.sharding import PartitionSpec as P


def from_root(value, axis, source):
    kept = jnp.where(lax.axis_index(axis) == source, value, 0).astype(value.dtype)
    return lax.psum(kept, axis)


def layer_norm(values, axis):
    values = values.astype(jnp.float32)
    average = jnp.mean(values, axis=axis, keepdims=True)
    centred = values - average
    variance = jnp.mean(centred * centred, axis=axis, keepdims=True)
    return centred * lax.rsqrt(variance + 1e-05)


def body(
    pair_rep,
    residue_mask,
    chain_index,
    mul_in,
    mul_gate,
    mul_out,
    att_in,
    att_bias,
    chain_bias,
    att_out,
    trans_up,
    trans_down,
):
    rows_here, cols_here, pair_width = pair_rep.shape
    row_pos = lax.axis_index("row")
    col_pos = lax.axis_index("col")
    col_ratio = lax.axis_size("col") // lax.axis_size("row")
    root_row = col_pos // col_ratio
    offset = col_pos % col_ratio * cols_here
    hidden_mul = mul_out.shape[0]
    head_count = att_bias.shape[1]
    attn_width = att_out.shape[0]
    head_dim = attn_width // head_count
    mask_all = residue_mask.astype(jnp.float32)
    row_mask = lax.dynamic_slice_in_dim(mask_all, row_pos * rows_here, rows_here)
    col_mask = lax.dynamic_slice_in_dim(mask_all, col_pos * cols_here, cols_here)
    chain_cols = lax.dynamic_slice_in_dim(chain_index, col_pos * cols_here, cols_here)
    normed = layer_norm(pair_rep, 2).astype(jnp.bfloat16)
    projected = jnp.einsum("ijp,pe->eij", normed, mul_in, preferred_element_type=jnp.float32)
    pair_mask = row_mask[:, None] * col_mask[None, :]
    left_proj = (
        pair_mask * jax.nn.sigmoid(projected[hidden_mul : 2 * hidden_mul]) * projected[:hidden_mul]
    ).astype(jnp.bfloat16)
    right_proj = (
        pair_mask
        * jax.nn.sigmoid(projected[3 * hidden_mul :])
        * projected[2 * hidden_mul : 3 * hidden_mul]
    ).astype(jnp.bfloat16)
    full_right = lax.all_gather(right_proj, "col", axis=2, tiled=True)
    picked = lax.dynamic_slice_in_dim(full_right, offset, cols_here, 1)
    right_panel = from_root(picked, "row", root_row)
    mix_sum = jnp.einsum(
        "cik,cjk->cij",
        lax.all_gather(left_proj, "col", axis=2, tiled=True),
        right_panel,
        preferred_element_type=jnp.float32,
    )
    mix_normed = layer_norm(mix_sum, 0).astype(jnp.bfloat16)
    gate_mul = jax.nn.sigmoid(
        jnp.einsum("ijp,pq->ijq", normed, mul_gate, preferred_element_type=jnp.float32)
    )
    update = gate_mul * jnp.einsum(
        "cij,cq->ijq", mix_normed, mul_out, preferred_element_type=jnp.float32
    )
    pair_one = (pair_rep.astype(jnp.float32) + update).astype(jnp.bfloat16)
    normed_two = layer_norm(pair_one, 2).astype(jnp.bfloat16)
    att_proj = jnp.einsum("ijp,pe->ije", normed_two, att_in, preferred_element_type=jnp.float32)
    queries = (
        att_proj[..., :attn_width]
        .astype(jnp.bfloat16)
        .reshape(rows_here, cols_here, head_count, head_dim)
    )
    gate_att = jax.nn.sigmoid(att_proj[..., 3 * attn_width :])
    bias_loc = jnp.einsum("ijp,ph->hij", normed_two, att_bias, preferred_element_type=jnp.float32)
    bias_rows = lax.all_gather(bias_loc, "col", axis=2, tiled=True)
    bias_pick = lax.dynamic_slice_in_dim(bias_rows, offset, cols_here, 1)
    bias_mine = from_root(bias_pick, "row", root_row)
    same_chain = (chain_cols[:, None] == chain_index[None, :]).astype(jnp.float32)
    bias_table = (
        bias_mine
        + chain_bias[:, None, None] * same_chain[None]
        + 1000000000.0 * (mask_all - 1.0)[None, None, :]
    )
    bias_table = jnp.transpose(bias_table, (1, 0, 2))
    score_scale = head_dim ** (-0.5)
    start_state = (
        jnp.full((rows_here, cols_here, head_count), -1e30, jnp.float32),
        jnp.zeros((rows_here, cols_here, head_count), jnp.float32),
        jnp.zeros((rows_here, cols_here, head_count, head_dim), jnp.float32),
    )
    key_loc = att_proj[..., attn_width : 2 * attn_width].astype(jnp.bfloat16)
    value_loc = att_proj[..., 2 * attn_width : 3 * attn_width].astype(jnp.bfloat16)
    segments = (
        lax.all_gather(key_loc, "col", axis=1, tiled=True),
        lax.all_gather(value_loc, "col", axis=1, tiled=True),
    )
    span = segments[0].shape[1]
    key_part = segments[0].reshape(rows_here, span, head_count, head_dim)
    value_part = segments[1].reshape(rows_here, span, head_count, head_dim)
    attend_span = key_part.shape[1]
    block_len = math.gcd(attend_span, 64)

    def advance(block_pos, state):
        top_score, denominator, weighted = state
        key_start = block_pos * block_len
        key_block = lax.dynamic_slice_in_dim(key_part, key_start, block_len, 1)
        value_block = lax.dynamic_slice_in_dim(value_part, key_start, block_len, 1)
        bias_block = lax.dynamic_slice_in_dim(bias_table, key_start, block_len, 2)
        scores = (
            jnp.einsum("ijhd,ikhd->ijhk", queries, key_block, preferred_element_type=jnp.float32)
            * score_scale
            + bias_block[None]
        )
        new_top = jnp.maximum(top_score, jnp.max(scores, axis=-1))
        rescale = jnp.exp(top_score - new_top)
        weights = jnp.exp(scores - new_top[..., None])
        denominator = denominator * rescale + jnp.sum(weights, axis=-1)
        weighted = weighted * rescale[..., None] + jnp.einsum(
            "ijhk,ikhd->ijhd",
            weights.astype(jnp.bfloat16),
            value_block,
            preferred_element_type=jnp.float32,
        )
        return (new_top, denominator, weighted)

    top_score, denominator, weighted = lax.fori_loop(
        0, attend_span // block_len, advance, start_state
    )
    attended = (weighted / denominator[..., None]).reshape(rows_here, cols_here, attn_width)
    gated_out = (gate_att * attended).astype(jnp.bfloat16)
    pair_two = (
        pair_one.astype(jnp.float32)
        + jnp.einsum("ije,eq->ijq", gated_out, att_out, preferred_element_type=jnp.float32)
    ).astype(jnp.bfloat16)
    normed_three = layer_norm(pair_two, 2).astype(jnp.bfloat16)
    inner_act = jax.nn.relu(
        jnp.einsum("ijp,pe->ije", normed_three, trans_up, preferred_element_type=jnp.float32)
    ).astype(jnp.bfloat16)
    return (
        pair_two.astype(jnp.float32)
        + jnp.einsum("ije,eq->ijq", inner_act, trans_down, preferred_element_type=jnp.float32)
    ).astype(jnp.bfloat16)


def solution(mesh):
    in_specs = (P("row", "col", None), P(), P(), P(), P(), P(), P(), P(), P(), P(), P(), P())
    out_specs = P("row", "col", None)
    return jax.shard_map(body, mesh=mesh, in_specs=in_specs, out_specs=out_specs, check_vma=False)
```

profile of v0, /device:TPU:1, one launch (start us, length us, event | category | flops | bytes accessed | tf_op | source)
XLA Modules:
  0.0 695.6 jit_solution(5081408751248228740)
XLA Ops:
  10.6 2.0 convolution_bitcast_fusion
  15.1 80.2 %all-gather.7.cloned.1.call-done = bf16[128,64,512]{0,2,1:T(8,128)(2,1)} async-done(((bf16[128,64,32]{0,2,1:T(8,128)(2,1)}), bf16[128,64,512]{0,2,1:T(8,128)(2,1)}) %all-gather.7.cloned.1.call-update) | async-done | bytes 8388624 | tf_op jit(solution)/shard_map/all_gather | solution.py:61
  95.3 4.4 dynamic-slice_select_fusion
  99.7 72.5 %all-gather.5.cloned.1.call-done = bf16[128,64,512]{0,2,1:T(8,128)(2,1)} async-done(((bf16[128,64,32]{0,2,1:T(8,128)(2,1)}), bf16[128,64,512]{0,2,1:T(8,128)(2,1)}) %all-gather.5.cloned.1.call-update) | async-done | bytes 8388624 | tf_op jit(solution)/shard_map/all_gather | solution.py:66
  172.2 29.1 %copy.67 = bf16[128,64,512]{1,2,0:T(8,128)(2,1)} copy(bf16[128,64,512]{0,2,1:T(8,128)(2,1)} %all-gather.5.cloned.1.call-done) | data formatting | bytes 16777216 | tf_op jit(solution)/shard_map/all_gather | solution.py:66
  201.4 75.6 %all-reduce.3.cloned.1.call-done = bf16[128,32,512]{0,2,1:T(8,128)(2,1)} async-done(((bf16[128,32,512]{0,2,1:T(8,128)(2,1)}), bf16[128,32,512]{0,2,1:T(8,128)(2,1)}) %all-reduce.3.cloned.1.call-update) | async-done | bytes 4194320 | tf_op jit(solution)/shard_map/psum | solution.py:11
  277.0 7.9 %copy.68 = bf16[128,32,512]{2,1,0:T(8,128)(2,1)} copy(bf16[128,32,512]{0,2,1:T(8,128)(2,1)} %all-reduce.3.cloned.1.call-done) | data formatting | bytes 8388608 | tf_op jit(solution)/shard_map/psum | solution.py:11
  284.9 9.7 %fusion.78 = (f32[64,32]{0,1:T(8,128)S(1)}, f32[128,64,32]{1,2,0:T(8,128)S(1)}) fusion(bf16[128,32,512]{2,1,0:T(8,128)(2,1)} %copy.68, bf16[128,64,512]{1,2,0:T(8,128)(2,1)} %copy.67), kind=kOutput, calls=%fused_computation.110 | convolution fusion | flops 268695552 | bytes 13639680 | tf_op jit(solution)/shard_map/cik,cjk->cij/dot_general | solution.py:64
  296.5 2.8 copy.73
  302.4 27.5 %all_gather.18 = f32[4,64,512]{1,0,2:T(4,128)S(1)} all-gather(f32[4,64,32]{1,0,2:T(4,128)S(1)} %copy.76), channel_id=1, replica_groups=mesh['row'=8,'col'=16] {'col'}, dimensions={2}, use_global_device_ids=true | all-gather | bytes 557056 | tf_op jit(solution)/shard_map/all_gather | solution.py:87
  331.9 2.5 fusion.79
  338.0 3.2 copy.79
  341.2 56.8 %all-reduce.5.cloned.1.call-done = f32[4,32,512]{1,0,2:T(4,128)} async-done(((f32[4,32,512]{1,0,2:T(4,128)}), f32[4,32,512]{1,0,2:T(4,128)}) %all-reduce.5.cloned.1.call-update) | async-done | bytes 262160 | tf_op jit(solution)/shard_map/psum | solution.py:11
  398.0 2.6 add_bitcast_fusion
  401.6 80.8 %all-gather.11.cloned.1.call-done = bf16[64,512,128]{2,1,0:T(8,128)(2,1)} async-done(((bf16[64,32,128]{2,1,0:T(8,128)(2,1)}), bf16[64,512,128]{2,1,0:T(8,128)(2,1)}) %all-gather.11.cloned.1.call-update) | async-done | bytes 8388624 | tf_op jit(solution)/shard_map/all_gather | solution.py:107
  482.5 12.0 %copy.78 = bf16[64,512,128]{1,2,0:T(8,128)(2,1)} copy(bf16[64,512,128]{2,1,0:T(8,128)(2,1)} %all-gather.11.cloned.1.call-done) | data formatting | bytes 16777216 | tf_op jit(solution)/shard_map/all_gather | solution.py:107
  494.5 64.8 %all-gather.9.cloned.1.call-done = bf16[64,512,128]{2,1,0:T(8,128)(2,1)} async-done(((bf16[64,32,128]{2,1,0:T(8,128)(2,1)}), bf16[64,512,128]{2,1,0:T(8,128)(2,1)}) %all-gather.9.cloned.1.call-update) | async-done | bytes 8388624 | tf_op jit(solution)/shard_map/all_gather | solution.py:106
  559.3 11.9 %copy.74 = bf16[64,512,128]{1,2,0:T(8,128)(2,1)} copy(bf16[64,512,128]{2,1,0:T(8,128)(2,1)} %all-gather.9.cloned.1.call-done) | data formatting | bytes 16777216 | tf_op jit(solution)/shard_map/all_gather | solution.py:106
  571.2 105.0 %while.18 = (s32[]{:T(128)}, f32[64,32,4]{1,2,0:T(4,128)S(1)}, f32[64,32,4]{1,2,0:T(4,128)S(1)}, f32[64,32,4,32]{1,3,2,0:T(8,128)}, bf16[64,512,4,32]{1,3,2,0:T(...) while((s32[]{:T(128)}, f32[64,32,4]{1,2,0:T(4,128)S(1)}, ...), condition=%wide.region_11.12_spmd.clone, body=%wide.region_8.11_spmd.clone.sunk | while | flops 73703424 | bytes 22184188 | solution.py:138
  572.1 3.4 fusion.93
  575.6 2.4 fusion.94
  578.2 4.2 bitcast_add_fusion.3
  582.4 1.9 copy-done.3
  585.2 3.4 fusion.93
  588.7 2.4 fusion.94
  591.3 4.2 bitcast_add_fusion.3
  595.5 1.9 copy-done.3
  598.4 3.4 fusion.93
  601.8 2.4 fusion.94
  604.4 4.2 bitcast_add_fusion.3
  611.5 3.4 fusion.93
  614.9 2.4 fusion.94
  617.5 4.2 bitcast_add_fusion.3
  624.6 3.4 fusion.93
  628.1 2.4 fusion.94
  630.7 4.2 bitcast_add_fusion.3
  637.7 3.4 fusion.93
  641.2 2.4 fusion.94
  643.8 4.2 bitcast_add_fusion.3
  650.9 3.4 fusion.93
  654.3 2.4 fusion.94
  656.9 4.2 bitcast_add_fusion.3
  664.0 3.4 fusion.93
  667.4 2.4 fusion.94
  670.0 4.2 bitcast_add_fusion.3
  676.2 5.0 broadcast_divide_fusion
  681.2 2.9 copy.82
  686.7 2.1 fusion.21
  (141 shorter events, 41.2 us)
Async XLA Ops:
  6.5 325.3 %copy-start = (bf16[128,512]{1,0:T(8,128)(2,1)S(1)}, bf16[128,512]{1,0:T(8,128)(2,1)}, u32[]{:S(2)}) copy-start(bf16[128,512]{1,0:T(8,128)(2,1)} %param.20) | copy-start | bytes 393220
  6.5 88.7 %all-gather.7.cloned.1.call-start = ((), (), s32[]{:S(2)}) async-start(), calls=%async_computation.1 | async-start | bytes 8912896 | tf_op jit(solution)/shard_map/all_gather | solution.py:61
  14.2 158.0 %all-gather.5.cloned.1.call-start = ((), (), s32[]{:S(2)}) async-start(), calls=%async_computation | async-start | bytes 8912896 | tf_op jit(solution)/shard_map/all_gather | solution.py:66
  15.0 262.0 %all-reduce.3.cloned.1.call-start = ((), (), s32[]{:S(2)}) async-start(), calls=%async_computation.2 | async-start | bytes 8388608 | tf_op jit(solution)/shard_map/psum | solution.py:11
  99.7 298.3 %all-reduce.5.cloned.1.call-start = ((), (), s32[]{:S(2)}) async-start(), calls=%async_computation.4 | async-start | bytes 2097152 | tf_op jit(solution)/shard_map/psum | solution.py:11
  294.5 4.8 copy-start.7
  294.7 4.9 copy-start.4
  294.7 4.9 copy-start.13
  299.3 2.1 copy-start.15
  300.8 33.6 %copy-start.5 = (bf16[64,32,128]{2,1,0:T(8,128)(2,1)}, bf16[64,32,128]{2,1,0:T(8,128)(2,1)S(1)}, u32[]{:S(2)}) copy-start(bf16[64,32,128]{2,1,0:T(8,128)(2,1)S(1)} %get-tuple-element.242) | copy-start | bytes 1572868
  331.6 4.6 copy-start.9
  331.6 5.6 copy-start.8
  331.7 150.8 %all-gather.11.cloned.1.call-start = ((), (), s32[]{:S(2)}) async-start(), calls=%async_computation.5 | async-start | bytes 8912896 | tf_op jit(solution)/shard_map/all_gather | solution.py:107
  334.4 63.6 %copy-start.10 = (f32[4]{0:T(128)S(1)}, f32[4]{0:T(128)}, u32[]{:S(2)}) copy-start(f32[4]{0:T(128)} %param.22) | copy-start | bytes 52
  335.7 223.6 %all-gather.9.cloned.1.call-start = ((), (), s32[]{:S(2)}) async-start(), calls=%async_computation.3 | async-start | bytes 8912896 | tf_op jit(solution)/shard_map/all_gather | solution.py:106
  575.5 2.7 copy-start.2
  582.4 1.9 copy-start.3
  588.6 2.7 copy-start.2
  595.5 1.9 copy-start.3
  601.7 2.7 copy-start.2
  608.6 1.9 copy-start.3
  614.9 2.7 copy-start.2
  621.8 1.9 copy-start.3
  628.0 2.7 copy-start.2
  634.9 1.9 copy-start.3
  641.1 2.7 copy-start.2
  648.0 1.9 copy-start.3
  654.2 2.7 copy-start.2
  661.1 1.9 copy-start.3
  667.4 2.7 copy-start.2
  674.3 1.9 copy-start.3
  681.2 2.9 copy-start.6
  681.2 2.9 copy-start.14
  684.1 2.6 copy-start.11
  684.1 2.6 copy-start.12
  684.1 4.7 copy-start.1
Sparse Core Ops, SparseCore 0:
  14.3 80.8 all-gather.6
  97.5 74.6 all-gather.4
  174.8 102.1 all-reduce.2
  331.7 66.2 all-reduce.4
  400.1 82.3 all-gather.10
  484.6 74.6 all-gather.8
where the time goes:
time: 698 us; the launch traced here: 696 us
  waiting for transfers between devices  432 us (62%)
  local copies, waits for them, and re-layouts  97 us (14%)
  matrix products  81.1 us (12%)
  other arithmetic  43.2 us (6%)
  blocking collectives  27.5 us (4%)
  between operations  13.8 us (2%)
    psum x2, waiting for transfers between devices, from_root(): return lax.psum(kept, axis)  132 us
    all_gather x1, waiting for transfers between devices, body(): lax.all_gather(value_loc, 'col', axis=1, tiled=True)  80.8 us
    all_gather x1, waiting for transfers between devices, body(): full_right = lax.all_gather(right_proj, 'col', axis=2, tiled=True)  80.2 us
    all_gather x1, waiting for transfers between devices, body(): lax.all_gather(left_proj, 'col', axis=2, tiled=True)  72.5 us
    all_gather x1, waiting for transfers between devices, body(): lax.all_gather(key_loc, 'col', axis=1, tiled=True)  64.8 us
    dot_general x8, matrix products, advance(): jnp.einsum('ijhk,ikhd->ijhd', weights.astype(jnp.bfloat16), value_block,...  33.8 us
    all_gather x1, local copies, waits for them, and re-layouts, body(): lax.all_gather(left_proj, 'col', axis=2, tiled=True)  29.1 us
    all_gather x1, blocking collectives, body(): bias_rows = lax.all_gather(bias_loc, 'col', axis=2, tiled=True)  27.5 us
  transfers between devices with their start and end apart: 6, of which 6 were waited for; matrix products, arithmetic and copies ran while one was open for 8% of the time, Pallas kernels for 0%

commit v1 on v0

v1 whole, which is shorter than its diff:
```python
import functools
import math

import jax
import jax.numpy as jnp
from jax import lax
from jax.experimental import pallas as pl
from jax.experimental.pallas import tpu as pltpu
from jax.sharding import PartitionSpec as P

MESH = pl.DeviceIdType.MESH
F32 = jnp.float32
BF16 = jnp.bfloat16
EPS = 1e-05
LOG2E = math.log2(math.e)
ORDERS = ((0, 1, 2), (1, 2, 0), (2, 0, 1))
UNITS = ((0, 3), (3, 3), (6, 2))


def norm(values, axis):
    centred = values - jnp.mean(values, axis=axis, keepdims=True)
    variance = jnp.mean(centred * centred, axis=axis, keepdims=True)
    return (centred * lax.rsqrt(variance + EPS)).astype(BF16)


def dot(a, b, ca=1, cb=0):
    return lax.dot_general(a, b, (((ca,), (cb,)), ((), ())), preferred_element_type=F32)


def one_hot(shape, hit):
    rows = lax.broadcasted_iota(jnp.int32, shape, 0)
    cols = lax.broadcasted_iota(jnp.int32, shape, 1)
    return jnp.where(hit(rows, cols), 1.0, 0.0).astype(BF16)


def kernel(
    pair_ref, mask_ref, chain_ref, mul_in_ref, mul_gate_ref, mul_out_ref, att_in_ref, att_bias_ref, chain_bias_ref,
    att_out_ref, up_ref, down_ref, out_ref,
    pair_f, lr_f, lr_s, lr_r, at_l, at_r, m_f, m_s, m_r, pair_rows, one_all, bias_own, bias0, bias1, bias2, table, same,
    keys, values, queries, gates, one_mine, out_s, out_r,
    ready, local, send, recv, gather_send, gather_recv,
):
    row, col = lax.axis_index("row"), lax.axis_index("col")
    me = row * 16 + col
    core = lax.rem(col, 2)
    place = (lax.rem(row, 4), col // 8 * 2 + row // 4, lax.rem(col // 2, 4))
    biases = (bias0, bias1, bias2)

    def device_at(c):
        return (lax.rem(c[1], 2) * 4 + c[0], c[1] // 2 * 8 + c[2] * 2 + core)

    def signal_row(sem):
        def one(s, carry):
            pl.semaphore_signal(sem, inc=1, device_id=(lax.rem(row + s, 8), col), device_id_type=MESH)
            return carry
        lax.fori_loop(1, 8, one, 0)

    def signal_col(sem):
        def one(s, carry):
            pl.semaphore_signal(sem, inc=1, device_id=(row, lax.rem(col + s, 16)), device_id_type=MESH)
            return carry
        lax.fori_loop(1, 16, one, 0)

    def remote(src, dst, which, target):
        return pltpu.make_async_remote_copy(src, dst, send.at[which], recv.at[which], device_id=target, device_id_type=MESH)

    barrier = pltpu.get_barrier_semaphore()
    signal_row(barrier)
    signal_col(barrier)

    mask = mask_ref[...].astype(F32)
    pair_f[...] = pair_ref[...].astype(F32).reshape(2048, 128)
    pick_rows = one_hot((512, 128), lambda a, b: a == row * 64 + lax.rem(b, 64))
    row_mask = dot(jnp.broadcast_to(mask, (16, 512)).astype(BF16), pick_rows)
    place_col = lax.broadcasted_iota(jnp.int32, (16, 512), 1) - (col * 32 + 2 * lax.broadcasted_iota(jnp.int32, (16, 512), 0))
    even = jnp.sum(jnp.where(place_col == 0, mask, 0.0), axis=1, keepdims=True)
    odd = jnp.sum(jnp.where(place_col == 1, mask, 0.0), axis=1, keepdims=True)
    lanes16 = lax.broadcasted_iota(jnp.int32, (16, 128), 1)
    pair_mask = jnp.where(lanes16 < 64, even, odd) * row_mask
    mul_in_t = mul_in_ref[...].T
    for step in range(8):
        parts = [pair_f[pl.ds(4 * step + u, 64, stride=32), :] for u in range(4)]
        normed = norm(jnp.concatenate(parts, axis=0).T, 0)
        projected = dot(mul_in_t, normed)
        masks = jnp.concatenate([pair_mask[2 * step : 2 * step + 1], pair_mask[2 * step + 1 : 2 * step + 2]], axis=1)
        left = masks * jax.nn.sigmoid(projected[128:256]) * projected[:128]
        right = masks * jax.nn.sigmoid(projected[384:]) * projected[256:384]
        for v in range(2):
            lr_f[pl.ds(2 * step + v, 128, stride=32), :] = left[:, v * 128 : v * 128 + 128]
            lr_f[pl.ds(16 + 2 * step + v, 128, stride=32), :] = right[:, v * 128 : v * 128 + 128]
    lr_s[...] = lr_f[...].reshape(128, 2, 16, 128).astype(BF16)

    pl.semaphore_wait(barrier, 22)
    signal_row(ready)
    pl.semaphore_wait(ready, 7)

    def to_all(src, dst, which):
        def one(s, carry):
            r, c = lax.rem(row + s // 16, 8), lax.rem(col + lax.rem(s, 16), 16)
            remote(src.at[r * 16 + c], dst.at[me], which, (r, c)).start()
            return carry
        lax.fori_loop(1, 128, one, 0)
        pltpu.make_async_copy(src.at[me], dst.at[me], local.at[which]).start()

    def all_here(src, dst, which):
        pltpu.make_async_copy(src.at[me], dst.at[me], local.at[which]).wait()
        whole = remote(src.at[pl.ds(0, 127)], dst.at[pl.ds(0, 127)], which, (row, col))
        whole.wait_send()
        whole.wait_recv()

    to_all(lr_s, lr_r, 0)

    def send_pair(s, carry):
        c = lax.rem(col + s, 16)
        remote(pair_ref.at[pl.ds(4 * c, 4)], pair_rows.at[col], 1, (row, c)).start()
        return carry
    lax.fori_loop(1, 16, send_pair, 0)
    pltpu.make_async_copy(pair_ref.at[pl.ds(4 * col, 4)], pair_rows.at[col], local.at[1]).start()

    def place_left(a, b):
        k, il, r, g = b // 128, lax.rem(b // 32, 4), lax.rem(b // 16, 2), lax.rem(b, 16)
        return a == r * 128 + k * 64 + 4 * g + il

    def place_right(a, b):
        k, r, i = b // 128, lax.rem(b // 64, 2), lax.rem(b, 64)
        return a == r * 128 + k * 64 + i

    orders = (one_hot((256, 256), place_left), one_hot((256, 256), place_right))
    head_rows = lax.broadcasted_iota(jnp.int32, (16, 512), 0)
    chains = jnp.where(head_rows == chain_ref[...], 1.0, 0.0).astype(BF16)
    mine = one_hot((256, 512), lambda a, b: b == a // 4 * 8 + core * 4 + lax.rem(a, 4))
    chains_mine = dot(chains, mine, 1, 1).astype(BF16)
    same[...] = dot(chains_mine.T, chains)

    all_here(lr_s, lr_r, 0)
    for side, at in ((0, at_l), (1, at_r)):
        for rp in range(4):
            here = [lr_r[(2 * rp + o) * 16 : (2 * rp + o + 1) * 16, side].reshape(256, 128) for o in range(2)]
            turned = dot(jnp.concatenate(here, axis=1), orders[side]).astype(BF16)
            at[0:256, rp * 128 : rp * 128 + 128] = turned[:, :128]
            at[256:512, rp * 128 : rp * 128 + 128] = turned[:, 128:]
    for rp in range(4):
        product = dot(at_l[:, rp * 128 : rp * 128 + 128].T, at_r[...])
        for il in range(4):
            for jt in range(4):
                m_f[pl.ds(rp * 512 + il * 4 + jt, 32, stride=16), :] = product[il * 32 : il * 32 + 32, jt * 128 : jt * 128 + 128]
    m_s[...] = m_f[...].reshape(128, 16, 128).astype(BF16)
    to_all(m_s, m_r, 2)

    pltpu.make_async_copy(pair_ref.at[pl.ds(0, 4)], pair_rows.at[0], local.at[1]).wait()
    whole = remote(pair_rows.at[pl.ds(0, 15)], pair_rows.at[pl.ds(0, 15)], 1, (row, col))
    whole.wait_send()
    whole.wait_recv()
    all_here(m_s, m_r, 2)

    m_f[...] = m_r[...].astype(F32).reshape(2048, 128)
    bias_in = jnp.concatenate([att_bias_ref[...].astype(F32).T, jnp.zeros((4, 128), F32)], axis=0).astype(BF16)
    for il in range(4):
        for jt in range(4):
            mix = norm(m_f[pl.ds(il * 4 + jt, 128, stride=16), :], 0)
            update = dot(mix, mul_out_ref[...], 0, 0)
            pair = pair_rows[4 * jt : 4 * jt + 4, il].reshape(128, 128).astype(F32)
            gate = jax.nn.sigmoid(dot(norm(pair, 1), mul_gate_ref[...]))
            one = (pair + gate * update).astype(BF16)
            one_all[core * 4 + il, jt * 128 : jt * 128 + 128] = one
            bias = dot(bias_in, norm(one.astype(F32), 1), 1, 1)
            for h in range(4):
                bias_own[h // 2 * 4 + jt, h % 2 * 4 + il : h % 2 * 4 + il + 1, :] = bias[h : h + 1]

    sibling = (row, col + 1 - 2 * core)
    swap = remote(one_all.at[pl.ds(core * 4, 4)], one_all.at[pl.ds(core * 4, 4)], 3, sibling)
    swap.start()

    def slab(o, phase, full):
        a, b, c = (place[axis] for axis in ORDERS[o])
        if phase == 0:
            return biases[o].at[c, b, pl.ds(0, 3)] if full else biases[o].at[c, b, a]
        if phase == 1:
            return biases[o].at[c, pl.ds(0, 3)] if full else biases[o].at[c, b]
        return biases[o].at[pl.ds(0, 3)] if full else biases[o].at[c]

    def gather_start(phase):
        for o in range(3):
            axis = ORDERS[o][phase]
            for s in (1, 3, 2):
                there = list(place)
                there[axis] = lax.rem(place[axis] + s, 4)
                ref = slab(o, phase, False)
                pltpu.make_async_remote_copy(
                    ref, ref, gather_send.at[o, phase], gather_recv.at[o, phase], device_id=device_at(there), device_id_type=MESH
                ).start()

    def gather_wait(phase):
        for o in range(3):
            ref = slab(o, phase, True)
            whole = pltpu.make_async_remote_copy(
                ref, ref, gather_send.at[o, phase], gather_recv.at[o, phase], device_id=(row, col), device_id_type=MESH
            )
            whole.wait_send()
            whole.wait_recv()

    for o in range(3):
        a, b, c = (place[axis] for axis in ORDERS[o])
        first, count = UNITS[o]
        biases[o][c, b, a] = bias_own[first : first + count]
    gather_start(0)

    heads = lax.broadcasted_iota(jnp.int32, (256, 128), 1) // 32

    def project(i):
        one = one_all[i]
        normed = norm(one.astype(F32), 1)
        normed_mine = dot(mine, normed).astype(BF16)
        one_mine[i] = dot(mine, one)
        kv = dot(normed, att_in_ref[:, 128:384]).astype(BF16)
        keys[i] = kv[:, :128]
        values[i] = kv[:, 128:]
        query = dot(normed_mine, att_in_ref[:, :128])
        for h in range(4):
            queries[i, h * 256 : h * 256 + 256] = jnp.where(heads == h, query, 0.0).astype(BF16)
        gates[i] = jax.nn.sigmoid(dot(normed_mine, att_in_ref[:, 384:]))

    def project_own(n, carry):
        project(core * 4 + n)
        return carry

    def project_other(n, carry):
        project(4 - core * 4 + n)
        return carry

    lax.fori_loop(0, 2, project_own, 0)
    gather_wait(0)
    gather_start(1)
    lax.fori_loop(2, 4, project_own, 0)
    gather_wait(1)
    gather_start(2)
    swap.wait()
    lax.fori_loop(0, 4, project_other, 0)
    gather_wait(2)

    mask_term = 1000000000.0 * (mask - 1.0)
    upper = lax.broadcasted_iota(jnp.int32, (8, 128), 0) < 4

    def build(n, carry):
        x, y = lax.rem(n // 2, 4), lax.rem(n, 2) * 2 + n // 8
        for u in range(8):
            o = 0 if u < 3 else 1 if u < 6 else 2
            lanes = pl.ds(u % 4 * 128, 128)
            for zp in range(2):
                tiles = []
                for z in (2 * zp, 2 * zp + 1):
                    at = (x, y, z)
                    a, b, c = (at[axis] for axis in ORDERS[o])
                    tiles.append(biases[o][c, b, a, u - UNITS[o][0]])
                rows = pl.ds(pl.multiple_of(n * 16 + zp * 8, 8), 8)
                together = same[rows, lanes]
                mixed = (
                    jnp.where(upper, tiles[0], pltpu.roll(tiles[1], 4, 0)),
                    jnp.where(upper, pltpu.roll(tiles[0], 4, 0), tiles[1]),
                )
                for h2 in range(2):
                    h = u // 4 * 2 + h2
                    value = mixed[h2] + chain_bias_ref[0, h] * together + mask_term[:, u % 4 * 128 : u % 4 * 128 + 128]
                    table[h, rows, lanes] = value * LOG2E
        return carry

    lax.fori_loop(0, 16, build, 0)

    scale = 32 ** (-0.5) * LOG2E

    def attend(i, carry):
        total = jnp.zeros((256, 128), F32)
        for h in range(4):
            scores = dot(queries[i, h * 256 : h * 256 + 256], keys[i], 1, 1) * scale + table[h]
            weights = jnp.exp2(scores - jnp.max(scores, axis=1, keepdims=True))
            denominator = jnp.sum(weights, axis=1, keepdims=True)
            weighted = dot(weights.astype(BF16), values[i])
            total = total + jnp.where(heads == h, weighted / denominator, 0.0)
        gated = (gates[i] * total).astype(BF16)
        two = (one_mine[i] + dot(gated, att_out_ref[...])).astype(BF16)
        two_f = two.astype(F32)
        inner = jnp.maximum(dot(norm(two_f, 1), up_ref[...]), 0.0).astype(BF16)
        result = (two_f + dot(inner, down_ref[...])).astype(BF16)
        out_s[:, i] = result.reshape(16, 16, 128)
        return carry

    lax.fori_loop(0, 8, attend, 0)

    def send_out(s, carry):
        c = lax.rem(col + s, 16)
        remote(out_s.at[c], out_r.at[col], 4, (row, c)).start()
        return carry
    lax.fori_loop(1, 16, send_out, 0)
    keep = pltpu.make_async_copy(out_s.at[col], out_r.at[col], local.at[4])
    keep.start()
    keep.wait()
    whole = remote(out_s.at[pl.ds(0, 15)], out_r.at[pl.ds(0, 15)], 4, (row, col))
    whole.wait_send()
    whole.wait_recv()

    def place_out(a, b):
        il, group, which, jl = a // 32, lax.rem(a // 8, 4), lax.rem(a // 4, 2), lax.rem(a, 4)
        return b == which * 128 + il * 16 + group * 4 + jl

    back = one_hot((256, 256), place_out)
    for chip in range(8):
        block = out_r[2 * chip : 2 * chip + 2].reshape(256, 128)
        out_ref[8 * chip : 8 * chip + 8] = dot(back, block).astype(BF16).reshape(8, 32, 128)


def body(pair_rep, residue_mask, chain_index, mul_in, mul_gate, mul_out, att_in, att_bias, chain_bias, att_out, trans_up, trans_down):
    vmem = pl.BlockSpec(memory_space=pltpu.VMEM)
    specs = [vmem] * 12
    specs[8] = pl.BlockSpec(memory_space=pltpu.SMEM)
    sem = pltpu.SemaphoreType
    return pl.pallas_call(
        kernel,
        out_shape=jax.ShapeDtypeStruct(pair_rep.shape, BF16),
        in_specs=specs,
        out_specs=vmem,
        scratch_shapes=[
            pltpu.VMEM((2048, 128), F32),
            pltpu.VMEM((4096, 128), F32),
            pltpu.VMEM((128, 2, 16, 128), BF16),
            pltpu.VMEM((128, 2, 16, 128), BF16),
            pltpu.VMEM((512, 512), BF16),
            pltpu.VMEM((512, 512), BF16),
            pltpu.VMEM((2048, 128), F32),
            pltpu.VMEM((128, 16, 128), BF16),
            pltpu.VMEM((128, 16, 128), BF16),
            pltpu.VMEM((16, 4, 32, 128), BF16),
            pltpu.VMEM((8, 512, 128), BF16),
            pltpu.VMEM((8, 8, 128), F32),
            pltpu.VMEM((4, 4, 4, 3, 8, 128), F32),
            pltpu.VMEM((4, 4, 4, 3, 8, 128), F32),
            pltpu.VMEM((4, 4, 4, 2, 8, 128), F32),
            pltpu.VMEM((4, 256, 512), F32),
            pltpu.VMEM((256, 512), F32),
            pltpu.VMEM((8, 512, 128), BF16),
            pltpu.VMEM((8, 512, 128), BF16),
            pltpu.VMEM((8, 1024, 128), BF16),
            pltpu.VMEM((8, 256, 128), F32),
            pltpu.VMEM((8, 256, 128), F32),
            pltpu.VMEM((16, 8, 16, 128), BF16),
            pltpu.VMEM((16, 8, 16, 128), BF16),
            sem.REGULAR,
            sem.DMA((5,)),
            sem.DMA((5,)),
            sem.DMA((5,)),
            sem.DMA((3, 3)),
            sem.DMA((3, 3)),
        ],
        compiler_params=pltpu.CompilerParams(collective_id=0, has_side_effects=True, vmem_limit_bytes=48 * 1024 * 1024),
    )(
        pair_rep, residue_mask.reshape(1, -1), chain_index.reshape(1, -1), mul_in, mul_gate, mul_out, att_in, att_bias,
        chain_bias.reshape(1, -1), att_out, trans_up, trans_down,
    )


def solution(mesh):
    in_specs = (P("row", "col", None),) + (P(),) * 11
    return jax.shard_map(body, mesh=mesh, in_specs=in_specs, out_specs=P("row", "col", None), check_vma=False)
```

time: 698 us -> 99.3 us (0.14)
  waiting for transfers between devices: 432 us -> 0 us
  Pallas kernels: 0 us -> 91 us
  local copies, waits for them, and re-layouts: 97 us -> 7.83 us
  matrix products: 81.1 us -> 0 us
  other arithmetic: 43.2 us -> 0 us
  blocking collectives: 27.5 us -> 0 us
  between operations: 13.8 us -> 0.06 us
    all_gather x4 -> x0, waiting for transfers between devices: 298 us -> none  [the longest x1 80.8 us: body(): lax.all_gather(value_loc, 'col', axis=1, tiled=True)]
    psum x2 -> x0, waiting for transfers between devices: 132 us -> none  [from_root(): return lax.psum(kept, axis)]
    pallas_call x0 -> x1, Pallas kernels: none -> 91 us  [body(): pl.pallas_call(kernel, out_shape=jax.ShapeDtypeStruct(pair_rep.shape, BF1...]
    dot_general x24 -> x0, matrix products: 81.1 us -> none  [the longest x8 33.8 us: advance(): jnp.einsum('ijhk,ikhd->ijhd', weights.astype(jnp.bfloat16), value_block,...]
    all_gather x3 -> x0, local copies, waits for them, and re-layouts: 53 us -> none  [the longest x1 29.1 us: body(): lax.all_gather(left_proj, 'col', axis=2, tiled=True)]
    all_gather x1 -> x0, blocking collectives: 27.5 us -> none  [body(): bias_rows = lax.all_gather(bias_loc, 'col', axis=2, tiled=True)]
    reduce_sum x13 -> x0, other arithmetic: 23.8 us -> none  [the longest x8 19.2 us: advance(): denominator = denominator * rescale + jnp.sum(weights, axis=-1)]
    while x40 -> x0, local copies, waits for them, and re-layouts: 15.3 us -> none
  transfers between devices with their start and end apart: 6 -> 0, of which waited for: 6 -> 0; matrix products, arithmetic and copies ran while one was open for 8% -> 0% of each run, Pallas kernels for 0% -> 0%
where the time goes in v1:
time: 99.3 us; the launch traced here: 98.8 us
  Pallas kernels  91 us (92%)
  local copies, waits for them, and re-layouts  7.83 us (8%)
    pallas_call x1, Pallas kernels, body(): pl.pallas_call(kernel, out_shape=jax.ShapeDtypeStruct(pair_rep.shape, BF1...  91 us
    unnamed x24, local copies, waits for them, and re-layouts  7.83 us

profile of v1, /device:TPU:1, one launch (start us, length us, event | category | flops | bytes accessed | tf_op | source)
XLA Modules:
  0.0 98.8 jit_solution(15252319132249669501)
XLA Ops:
  0.0 0.0 copy-start.5
  0.0 0.0 copy-start.8
  0.0 0.0 copy-start.9
  0.0 0.0 copy-start.10
  0.0 0.9 copy.13.att_bias_ref
  0.9 0.0 copy-done.5
  0.9 0.0 copy-done.8
  0.9 0.0 copy-done.9
  0.9 0.0 copy-done.10
  0.9 0.0 copy-start
  0.9 1.0 %copy-done = bf16[64,32,128]{2,1,0:T(8,128)(2,1)S(1)} copy-done((bf16[64,32,128]{2,1,0:T(8,128)(2,1)S(1)}, bf16[64,32,128]{2,1,0:T(8,128)(2,1)}, u32[]{:S(2)}) %copy-start) | copy-done | bytes 524312
  1.9 0.0 copy-start.1
  1.9 0.9 copy-done.1
  2.9 0.0 copy-start.2
  2.9 0.9 copy-done.2
  3.8 0.0 copy-start.3
  3.8 0.9 copy-done.3
  4.7 0.0 copy-start.4
  4.7 0.9 copy-done.4
  5.6 0.0 copy-start.6
  5.6 0.8 copy-done.6
  6.3 0.0 copy-start.7
  6.3 0.8 copy-done.7
  7.1 91.0 %shard_map.118 = bf16[64,32,128]{2,1,0:T(8,128)(2,1)S(1)} custom-call(bf16[64,32,128]{2,1,0:T(8,128)(2,1)S(1)} %copy-done, s32[1,512]{1,0:T(1,128)S(1)} %bitcast.3, s32[1,512]{1,0:T(1,128)S(1)} %bitcast.4, bf16[128,512]{1,0:T(8,128)(2,1)S(1)} %copy-done.1, bf16[128,128]{1,0:T(8,128)(2,1)S(1)} %copy-done.5, bf16[128,128]{1,0:T(8,128)(2,1)S(1)} %copy-done.6, ...), custom_call_target="tpu_custom_call" | custom-call | tf_op jit(solution)/shard_map/pallas_call | solution.py:316
  98.0 0.8 copy.15
Async XLA Ops:
  0.0 0.9 copy-start.5
  0.0 0.9 copy-start.8
  0.0 0.9 copy-start.9
  0.0 0.9 copy-start.10
  0.9 1.0 %copy-start = (bf16[64,32,128]{2,1,0:T(8,128)(2,1)S(1)}, bf16[64,32,128]{2,1,0:T(8,128)(2,1)}, u32[]{:S(2)}) copy-start(bf16[64,32,128]{2,1,0:T(8,128)(2,1)} %pair_ref.1) | copy-start | bytes 1572868
  1.9 0.9 copy-start.1
  2.9 0.9 copy-start.2
  3.8 0.9 copy-start.3
  4.7 0.9 copy-start.4
  5.6 0.8 copy-start.6
  6.3 0.8 copy-start.7

commit v2 on v1

--- a/solution.py
+++ b/solution.py
@@ -13,8 +13,8 @@
 BF16 = jnp.bfloat16
 EPS = 1e-05
 LOG2E = math.log2(math.e)
-ORDERS = ((0, 1, 2), (1, 2, 0), (2, 0, 1))
-UNITS = ((0, 3), (3, 3), (6, 2))
+ORDERS = ((0, 1, 2), (1, 2, 0), (2, 0, 1), (0, 1, 2), (1, 2, 0))
+OUT_ROWS = ((0, 4), (4, 2), (6, 2))
 
 
 def norm(values, axis):
@@ -34,17 +34,18 @@
 
 
 def kernel(
-    pair_ref, mask_ref, chain_ref, mul_in_ref, mul_gate_ref, mul_out_ref, att_in_ref, att_bias_ref, chain_bias_ref,
-    att_out_ref, up_ref, down_ref, out_ref,
-    pair_f, lr_f, lr_s, lr_r, at_l, at_r, m_f, m_s, m_r, pair_rows, one_all, bias_own, bias0, bias1, bias2, table, same,
-    keys, values, queries, gates, one_mine, out_s, out_r,
-    ready, local, send, recv, gather_send, gather_recv,
+    pair_in, mask_in, chain_in, mul_in_in, mul_gate_in, mul_out_in, att_in_in, att_bias_in, chain_bias_ref,
+    att_out_in, up_in, down_in, out_ref,
+    pair_ref, mask_ref, chain_ref, mul_in_ref, mul_gate_ref, mul_out_ref, att_in_ref, att_bias_ref, att_out_ref, up_ref, down_ref,
+    pair_f, lr_f, lr_s, lr_r, at_l, at_r, m_f, m_s, m_r, pair_rows, one_all, bias0, bias1, bias2, bias3, bias4, table, same,
+    keys, values, queries, gates, one_mine, score_s, weight_s, total_s, out_s, out_r,
+    ready, load, local, send, recv, gather_send, gather_recv,
 ):
     row, col = lax.axis_index("row"), lax.axis_index("col")
     me = row * 16 + col
     core = lax.rem(col, 2)
     place = (lax.rem(row, 4), col // 8 * 2 + row // 4, lax.rem(col // 2, 4))
-    biases = (bias0, bias1, bias2)
+    biases = (bias0, bias1, bias2, bias3, bias4)
 
     def device_at(c):
         return (lax.rem(c[1], 2) * 4 + c[0], c[1] // 2 * 8 + c[2] * 2 + core)
@@ -64,9 +65,23 @@
     def remote(src, dst, which, target):
         return pltpu.make_async_remote_copy(src, dst, send.at[which], recv.at[which], device_id=target, device_id_type=MESH)
 
+    loads = [
+        pltpu.make_async_copy(src, dst, load.at[n])
+        for n, (src, dst) in enumerate((
+            (mask_in, mask_ref), (pair_in, pair_ref), (mul_in_in, mul_in_ref), (chain_in, chain_ref),
+            (mul_gate_in, mul_gate_ref), (mul_out_in, mul_out_ref), (att_in_in, att_in_ref), (att_bias_in, att_bias_ref),
+            (att_out_in, att_out_ref), (up_in, up_ref), (down_in, down_ref),
+        ))
+    ]
+    for one in loads[:3]:
+        one.start()
     barrier = pltpu.get_barrier_semaphore()
     signal_row(barrier)
     signal_col(barrier)
+    for one in loads[3:]:
+        one.start()
+    for one in loads[:3]:
+        one.wait()
 
     mask = mask_ref[...].astype(F32)
     pair_f[...] = pair_ref[...].astype(F32).reshape(2048, 128)
@@ -79,6 +94,9 @@
     pair_mask = jnp.where(lanes16 < 64, even, odd) * row_mask
     mul_in_t = mul_in_ref[...].T
     for step in range(8):
+        if step == 4:
+            pl.semaphore_wait(barrier, 22)
+            signal_row(ready)
         parts = [pair_f[pl.ds(4 * step + u, 64, stride=32), :] for u in range(4)]
         normed = norm(jnp.concatenate(parts, axis=0).T, 0)
         projected = dot(mul_in_t, normed)
@@ -90,8 +108,8 @@
             lr_f[pl.ds(16 + 2 * step + v, 128, stride=32), :] = right[:, v * 128 : v * 128 + 128]
     lr_s[...] = lr_f[...].reshape(128, 2, 16, 128).astype(BF16)
 
-    pl.semaphore_wait(barrier, 22)
-    signal_row(ready)
+    for one in loads[3:]:
+        one.wait()
     pl.semaphore_wait(ready, 7)
 
     def to_all(src, dst, which):
@@ -110,6 +128,23 @@
 
     to_all(lr_s, lr_r, 0)
 
+    def place_left(a, b):
+        k, il, r, g = b // 128, lax.rem(b // 32, 4), lax.rem(b // 16, 2), lax.rem(b, 16)
+        return a == r * 128 + k * 64 + 4 * g + il
+
+    def place_right(a, b):
+        k, r, i = b // 128, lax.rem(b // 64, 2), lax.rem(b, 64)
+        return a == r * 128 + k * 64 + i
+
+    orders = (one_hot((256, 256), place_left), one_hot((256, 256), place_right))
+    head_rows = lax.broadcasted_iota(jnp.int32, (16, 512), 0)
+    chains = jnp.where(head_rows == chain_ref[...], 1.0, 0.0).astype(BF16)
+    mine = one_hot((256, 512), lambda a, b: b == a // 4 * 8 + core * 4 + lax.rem(a, 4))
+    chains_mine = dot(chains, mine, 1, 1).astype(BF16)
+    same[...] = dot(chains_mine.T, chains)
+
+    all_here(lr_s, lr_r, 0)
+
     def send_pair(s, carry):
         c = lax.rem(col + s, 16)
         remote(pair_ref.at[pl.ds(4 * c, 4)], pair_rows.at[col], 1, (row, c)).start()
@@ -117,22 +152,6 @@
     lax.fori_loop(1, 16, send_pair, 0)
     pltpu.make_async_copy(pair_ref.at[pl.ds(4 * col, 4)], pair_rows.at[col], local.at[1]).start()
 
-    def place_left(a, b):
-        k, il, r, g = b // 128, lax.rem(b // 32, 4), lax.rem(b // 16, 2), lax.rem(b, 16)
-        return a == r * 128 + k * 64 + 4 * g + il
-
-    def place_right(a, b):
-        k, r, i = b // 128, lax.rem(b // 64, 2), lax.rem(b, 64)
-        return a == r * 128 + k * 64 + i
-
-    orders = (one_hot((256, 256), place_left), one_hot((256, 256), place_right))
-    head_rows = lax.broadcasted_iota(jnp.int32, (16, 512), 0)
-    chains = jnp.where(head_rows == chain_ref[...], 1.0, 0.0).astype(BF16)
-    mine = one_hot((256, 512), lambda a, b: b == a // 4 * 8 + core * 4 + lax.rem(a, 4))
-    chains_mine = dot(chains, mine, 1, 1).astype(BF16)
-    same[...] = dot(chains_mine.T, chains)
-
-    all_here(lr_s, lr_r, 0)
     for side, at in ((0, at_l), (1, at_r)):
         for rp in range(4):
             here = [lr_r[(2 * rp + o) * 16 : (2 * rp + o + 1) * 16, side].reshape(256, 128) for o in range(2)]
@@ -151,25 +170,15 @@
     whole = remote(pair_rows.at[pl.ds(0, 15)], pair_rows.at[pl.ds(0, 15)], 1, (row, col))
     whole.wait_send()
     whole.wait_recv()
+
+    def pair_tile(jt, il):
+        return pair_rows[4 * jt : 4 * jt + 4, il].reshape(128, 128).astype(F32)
+
+    for jt in range(4):
+        for il in range(4):
+            at = (il * 4 + jt) * 128
+            pair_f[at : at + 128] = jax.nn.sigmoid(dot(norm(pair_tile(jt, il), 1), mul_gate_ref[...]))
     all_here(m_s, m_r, 2)
-
-    m_f[...] = m_r[...].astype(F32).reshape(2048, 128)
-    bias_in = jnp.concatenate([att_bias_ref[...].astype(F32).T, jnp.zeros((4, 128), F32)], axis=0).astype(BF16)
-    for il in range(4):
-        for jt in range(4):
-            mix = norm(m_f[pl.ds(il * 4 + jt, 128, stride=16), :], 0)
-            update = dot(mix, mul_out_ref[...], 0, 0)
-            pair = pair_rows[4 * jt : 4 * jt + 4, il].reshape(128, 128).astype(F32)
-            gate = jax.nn.sigmoid(dot(norm(pair, 1), mul_gate_ref[...]))
-            one = (pair + gate * update).astype(BF16)
-            one_all[core * 4 + il, jt * 128 : jt * 128 + 128] = one
-            bias = dot(bias_in, norm(one.astype(F32), 1), 1, 1)
-            for h in range(4):
-                bias_own[h // 2 * 4 + jt, h % 2 * 4 + il : h % 2 * 4 + il + 1, :] = bias[h : h + 1]
-
-    sibling = (row, col + 1 - 2 * core)
-    swap = remote(one_all.at[pl.ds(core * 4, 4)], one_all.at[pl.ds(core * 4, 4)], 3, sibling)
-    swap.start()
 
     def slab(o, phase, full):
         a, b, c = (place[axis] for axis in ORDERS[o])
@@ -179,10 +188,12 @@
             return biases[o].at[c, pl.ds(0, 3)] if full else biases[o].at[c, b]
         return biases[o].at[pl.ds(0, 3)] if full else biases[o].at[c]
 
-    def gather_start(phase):
-        for o in range(3):
-            axis = ORDERS[o][phase]
-            for s in (1, 3, 2):
+    early, late = (0, 1, 2), (3, 4)
+
+    def gather_start(phase, which):
+        for s in (1, 3, 2):
+            for o in which:
+                axis = ORDERS[o][phase]
                 there = list(place)
                 there[axis] = lax.rem(place[axis] + s, 4)
                 ref = slab(o, phase, False)
@@ -190,8 +201,8 @@
                     ref, ref, gather_send.at[o, phase], gather_recv.at[o, phase], device_id=device_at(there), device_id_type=MESH
                 ).start()
 
-    def gather_wait(phase):
-        for o in range(3):
+    def gather_wait(phase, which):
+        for o in which:
             ref = slab(o, phase, True)
             whole = pltpu.make_async_remote_copy(
                 ref, ref, gather_send.at[o, phase], gather_recv.at[o, phase], device_id=(row, col), device_id_type=MESH
@@ -199,11 +210,26 @@
             whole.wait_send()
             whole.wait_recv()
 
-    for o in range(3):
-        a, b, c = (place[axis] for axis in ORDERS[o])
-        first, count = UNITS[o]
-        biases[o][c, b, a] = bias_own[first : first + count]
-    gather_start(0)
+    m_f[...] = m_r[...].astype(F32).reshape(2048, 128)
+    bias_in = jnp.concatenate([att_bias_ref[...].astype(F32), jnp.zeros((4, 128), F32)], axis=0).astype(BF16)
+    for jt in range(4):
+        for il in range(4):
+            at = il * 4 + jt
+            mix = norm(m_f[pl.ds(at, 128, stride=16), :], 0)
+            update = dot(mix, mul_out_ref[...], 0, 0)
+            one = (pair_tile(jt, il) + pair_f[at * 128 : at * 128 + 128] * update).astype(BF16)
+            one_all[core * 4 + il, jt * 128 : jt * 128 + 128] = one
+            bias = dot(bias_in, norm(one.astype(F32), 1), 1, 1)
+            for h in range(4):
+                o, slot = (jt, h // 2) if jt < 3 else (3 + h // 2, 0)
+                a, b, c = (place[axis] for axis in ORDERS[o])
+                biases[o][c, b, a, slot, h % 2 * 4 + il : h % 2 * 4 + il + 1, :] = bias[h : h + 1]
+        if jt == 2:
+            gather_start(0, early)
+    gather_start(0, late)
+    sibling = (row, col + 1 - 2 * core)
+    swap = remote(one_all.at[pl.ds(core * 4, 4)], one_all.at[pl.ds(core * 4, 4)], 3, sibling)
+    swap.start()
 
     heads = lax.broadcasted_iota(jnp.int32, (256, 128), 1) // 32
 
@@ -229,14 +255,17 @@
         return carry
 
     lax.fori_loop(0, 2, project_own, 0)
-    gather_wait(0)
-    gather_start(1)
+    for group in (early, late):
+        gather_wait(0, group)
+        gather_start(1, group)
     lax.fori_loop(2, 4, project_own, 0)
-    gather_wait(1)
-    gather_start(2)
+    for group in (early, late):
+        gather_wait(1, group)
+        gather_start(2, group)
     swap.wait()
     lax.fori_loop(0, 4, project_other, 0)
-    gather_wait(2)
+    gather_wait(2, early)
+    gather_wait(2, late)
 
     mask_term = 1000000000.0 * (mask - 1.0)
     upper = lax.broadcasted_iota(jnp.int32, (8, 128), 0) < 4
@@ -244,14 +273,15 @@
     def build(n, carry):
         x, y = lax.rem(n // 2, 4), lax.rem(n, 2) * 2 + n // 8
         for u in range(8):
-            o = 0 if u < 3 else 1 if u < 6 else 2
+            hp, kt = u // 4, u % 4
+            o, slot = (kt, hp) if kt < 3 else (3 + hp, 0)
             lanes = pl.ds(u % 4 * 128, 128)
             for zp in range(2):
                 tiles = []
                 for z in (2 * zp, 2 * zp + 1):
                     at = (x, y, z)
                     a, b, c = (at[axis] for axis in ORDERS[o])
-                    tiles.append(biases[o][c, b, a, u - UNITS[o][0]])
+                    tiles.append(biases[o][c, b, a, slot])
                 rows = pl.ds(pl.multiple_of(n * 16 + zp * 8, 8), 8)
                 together = same[rows, lanes]
                 mixed = (
@@ -268,35 +298,58 @@
 
     scale = 32 ** (-0.5) * LOG2E
 
-    def attend(i, carry):
+    def score(i, slot):
+        score_s[slot] = dot(queries[i], keys[i], 1, 1)
+
+    def soften(slot):
+        for n in range(16):
+            rows = slice(n * 64, n * 64 + 64)
+            scores = score_s[slot, rows] * scale + table[n // 4, n % 4 * 64 : n % 4 * 64 + 64]
+            weights = jnp.exp2(scores - jnp.max(scores, axis=1, keepdims=True))
+            total_s[slot, rows] = jnp.broadcast_to(jnp.sum(weights, axis=1, keepdims=True), (64, 128))
+            weight_s[slot, rows] = weights.astype(BF16)
+
+    def finish(i, slot):
+        weighted = dot(weight_s[slot], values[i]) / total_s[slot]
         total = jnp.zeros((256, 128), F32)
         for h in range(4):
-            scores = dot(queries[i, h * 256 : h * 256 + 256], keys[i], 1, 1) * scale + table[h]
-            weights = jnp.exp2(scores - jnp.max(scores, axis=1, keepdims=True))
-            denominator = jnp.sum(weights, axis=1, keepdims=True)
-            weighted = dot(weights.astype(BF16), values[i])
-            total = total + jnp.where(heads == h, weighted / denominator, 0.0)
+            total = total + jnp.where(heads == h, weighted[h * 256 : h * 256 + 256], 0.0)
         gated = (gates[i] * total).astype(BF16)
         two = (one_mine[i] + dot(gated, att_out_ref[...])).astype(BF16)
         two_f = two.astype(F32)
         inner = jnp.maximum(dot(norm(two_f, 1), up_ref[...]), 0.0).astype(BF16)
         result = (two_f + dot(inner, down_ref[...])).astype(BF16)
         out_s[:, i] = result.reshape(16, 16, 128)
-        return carry
-
-    lax.fori_loop(0, 8, attend, 0)
-
-    def send_out(s, carry):
-        c = lax.rem(col + s, 16)
-        remote(out_s.at[c], out_r.at[col], 4, (row, c)).start()
-        return carry
-    lax.fori_loop(1, 16, send_out, 0)
-    keep = pltpu.make_async_copy(out_s.at[col], out_r.at[col], local.at[4])
-    keep.start()
-    keep.wait()
-    whole = remote(out_s.at[pl.ds(0, 15)], out_r.at[pl.ds(0, 15)], 4, (row, col))
-    whole.wait_send()
-    whole.wait_recv()
+
+    def send_out(part):
+        first, count = OUT_ROWS[part]
+        rows = pl.ds(first, count)
+
+        def one(s, carry):
+            c = lax.rem(col + s, 16)
+            remote(out_s.at[c, rows], out_r.at[col, rows], 4 + part, (row, c)).start()
+            return carry
+        lax.fori_loop(1, 16, one, 0)
+        pltpu.make_async_copy(out_s.at[col, rows], out_r.at[col, rows], local.at[4 + part]).start()
+
+    score(0, 0)
+    for i in range(8):
+        if i < 7:
+            score(i + 1, (i + 1) % 2)
+        soften(i % 2)
+        if i > 0:
+            finish(i - 1, (i - 1) % 2)
+        for part in range(2):
+            if i == OUT_ROWS[part + 1][0]:
+                send_out(part)
+    finish(7, 1)
+    send_out(2)
+    for part in range(3):
+        rows = pl.ds(*OUT_ROWS[part])
+        pltpu.make_async_copy(out_s.at[col, rows], out_r.at[col, rows], local.at[4 + part]).wait()
+        whole = remote(out_s.at[pl.ds(0, 15), rows], out_r.at[pl.ds(0, 15), rows], 4 + part, (row, col))
+        whole.wait_send()
+        whole.wait_recv()
 
     def place_out(a, b):
         il, group, which, jl = a // 32, lax.rem(a // 8, 4), lax.rem(a // 4, 2), lax.rem(a, 4)
@@ -310,15 +363,20 @@
 
 def body(pair_rep, residue_mask, chain_index, mul_in, mul_gate, mul_out, att_in, att_bias, chain_bias, att_out, trans_up, trans_down):
     vmem = pl.BlockSpec(memory_space=pltpu.VMEM)
-    specs = [vmem] * 12
+    specs = [pl.BlockSpec(memory_space=pl.ANY)] * 12
     specs[8] = pl.BlockSpec(memory_space=pltpu.SMEM)
     sem = pltpu.SemaphoreType
+    args = (
+        pair_rep, residue_mask.reshape(1, -1), chain_index.reshape(1, -1), mul_in, mul_gate, mul_out, att_in, att_bias.T,
+        chain_bias.reshape(1, -1), att_out, trans_up, trans_down,
+    )
     return pl.pallas_call(
         kernel,
         out_shape=jax.ShapeDtypeStruct(pair_rep.shape, BF16),
         in_specs=specs,
         out_specs=vmem,
-        scratch_shapes=[
+        scratch_shapes=[pltpu.VMEM(a.shape, a.dtype) for n, a in enumerate(args) if n != 8]
+        + [
             pltpu.VMEM((2048, 128), F32),
             pltpu.VMEM((4096, 128), F32),
             pltpu.VMEM((128, 2, 16, 128), BF16),
@@ -330,10 +388,11 @@
             pltpu.VMEM((128, 16, 128), BF16),
             pltpu.VMEM((16, 4, 32, 128), BF16),
             pltpu.VMEM((8, 512, 128), BF16),
-            pltpu.VMEM((8, 8, 128), F32),
-            pltpu.VMEM((4, 4, 4, 3, 8, 128), F32),
-            pltpu.VMEM((4, 4, 4, 3, 8, 128), F32),
             pltpu.VMEM((4, 4, 4, 2, 8, 128), F32),
+            pltpu.VMEM((4, 4, 4, 2, 8, 128), F32),
+            pltpu.VMEM((4, 4, 4, 2, 8, 128), F32),
+            pltpu.VMEM((4, 4, 4, 1, 8, 128), F32),
+            pltpu.VMEM((4, 4, 4, 1, 8, 128), F32),
             pltpu.VMEM((4, 256, 512), F32),
             pltpu.VMEM((256, 512), F32),
             pltpu.VMEM((8, 512, 128), BF16),
@@ -341,20 +400,21 @@
             pltpu.VMEM((8, 1024, 128), BF16),
             pltpu.VMEM((8, 256, 128), F32),
             pltpu.VMEM((8, 256, 128), F32),
+            pltpu.VMEM((2, 1024, 512), F32),
+            pltpu.VMEM((2, 1024, 512), BF16),
+            pltpu.VMEM((2, 1024, 128), F32),
             pltpu.VMEM((16, 8, 16, 128), BF16),
             pltpu.VMEM((16, 8, 16, 128), BF16),
             sem.REGULAR,
-            sem.DMA((5,)),
-            sem.DMA((5,)),
-            sem.DMA((5,)),
-            sem.DMA((3, 3)),
-            sem.DMA((3, 3)),
+            sem.DMA((11,)),
+            sem.DMA((7,)),
+            sem.DMA((7,)),
+            sem.DMA((7,)),
+            sem.DMA((5, 3)),
+            sem.DMA((5, 3)),
         ],
-        compiler_params=pltpu.CompilerParams(collective_id=0, has_side_effects=True, vmem_limit_bytes=48 * 1024 * 1024),
-    )(
-        pair_rep, residue_mask.reshape(1, -1), chain_index.reshape(1, -1), mul_in, mul_gate, mul_out, att_in, att_bias,
-        chain_bias.reshape(1, -1), att_out, trans_up, trans_down,
-    )
+        compiler_params=pltpu.CompilerParams(collective_id=0, has_side_effects=True, vmem_limit_bytes=56 * 1024 * 1024),
+    )(*args)
 
 
 def solution(mesh):

time: 99.3 us -> 87.8 us (0.88)
  local copies, waits for them, and re-layouts: 7.83 us -> 1.87 us
  Pallas kernels: 91 us -> 85.7 us
    unnamed x24 -> x1, local copies, waits for them, and re-layouts: 7.83 us -> 1.87 us
    pallas_call x1, Pallas kernels: 91 us -> 85.7 us  [body(): pl.pallas_call(kernel, out_shape=jax.ShapeDtypeStruct(pair_rep.shape, BF1...]
where the time goes in v2:
time: 87.8 us; the launch traced here: 87.6 us
  Pallas kernels  85.7 us (98%)
  local copies, waits for them, and re-layouts  1.87 us (2%)
    pallas_call x1, Pallas kernels, body(): pl.pallas_call(kernel, out_shape=jax.ShapeDtypeStruct(pair_rep.shape, BF1...  85.7 us
    unnamed x1, local copies, waits for them, and re-layouts  1.87 us

profile of v2, /device:TPU:1, one launch (start us, length us, event | category | flops | bytes accessed | tf_op | source)
XLA Modules:
  0.0 87.6 jit_solution(17006652871604972355)
XLA Ops:
  0.0 85.7 %shard_map.118 = bf16[64,32,128]{2,1,0:T(8,128)(2,1)} custom-call(bf16[64,32,128]{2,1,0:T(8,128)(2,1)} %pair_in.1, s32[1,512]{1,0:T(1,128)} %bitcast.4, s32[1,512]{1,0:T(1,128)} %bitcast.5, bf16[128,512]{1,0:T(8,128)(2,1)} %mul_in_in.1, bf16[128,128]{1,0:T(8,128)(2,1)} %mul_gate_in.1, bf16[128,128]{1,0:T(8,128)(2,1)} %mul_out_in.1, ...), custom_call_target="tpu_custom_call" | custom-call | tf_op jit(solution)/shard_map/pallas_call | solution.py:373
  85.8 1.9 %copy.14 = bf16[64,32,128]{2,1,0:T(8,128)(2,1)} copy(bf16[64,32,128]{2,1,0:T(8,128)(2,1)} %shard_map.118) | data formatting | bytes 1048576

commit v3 on v2

--- a/solution.py
+++ b/solution.py
@@ -13,8 +13,8 @@
 BF16 = jnp.bfloat16
 EPS = 1e-05
 LOG2E = math.log2(math.e)
-ORDERS = ((0, 1, 2), (1, 2, 0), (2, 0, 1), (0, 1, 2), (1, 2, 0))
-OUT_ROWS = ((0, 4), (4, 2), (6, 2))
+ORDERS = ((0, 1, 2), (1, 2, 0), (2, 0, 1), (1, 2, 0), (0, 1, 2), (2, 0, 1))
+WHERE = {(0, 0): (0, 0), (1, 0): (0, 1), (0, 1): (1, 0), (1, 1): (2, 0), (0, 2): (3, 0), (1, 2): (3, 1), (0, 3): (4, 0), (1, 3): (5, 0)}
 
 
 def norm(values, axis):
@@ -37,15 +37,15 @@
     pair_in, mask_in, chain_in, mul_in_in, mul_gate_in, mul_out_in, att_in_in, att_bias_in, chain_bias_ref,
     att_out_in, up_in, down_in, out_ref,
     pair_ref, mask_ref, chain_ref, mul_in_ref, mul_gate_ref, mul_out_ref, att_in_ref, att_bias_ref, att_out_ref, up_ref, down_ref,
-    pair_f, lr_f, lr_s, lr_r, at_l, at_r, m_f, m_s, m_r, pair_rows, one_all, bias0, bias1, bias2, bias3, bias4, table, same,
-    keys, values, queries, gates, one_mine, score_s, weight_s, total_s, out_s, out_r,
+    pair_f, lr_f, lr_s, lr_r, at_l, at_r, m_f, m_s, m_r, pair_rows, one_all, normed_all, bias0, bias1, bias2, bias3, bias4, bias5, table, same,
+    keys, values, queries, gates, one_mine, score_s, weight_s, total_s, gated_s, out_s, out_r,
     ready, load, local, send, recv, gather_send, gather_recv,
 ):
     row, col = lax.axis_index("row"), lax.axis_index("col")
     me = row * 16 + col
     core = lax.rem(col, 2)
     place = (lax.rem(row, 4), col // 8 * 2 + row // 4, lax.rem(col // 2, 4))
-    biases = (bias0, bias1, bias2, bias3, bias4)
+    biases = (bias0, bias1, bias2, bias3, bias4, bias5)
 
     def device_at(c):
         return (lax.rem(c[1], 2) * 4 + c[0], c[1] // 2 * 8 + c[2] * 2 + core)
@@ -83,6 +83,16 @@
     for one in loads[:3]:
         one.wait()
 
+    def send_pair(part):
+        rows = pl.ds(2 * part, 2)
+
+        def one(s, carry):
+            c = lax.rem(col + s, 16)
+            remote(pair_ref.at[pl.ds(4 * c + 2 * part, 2)], pair_rows.at[col, rows], 6 + part, (row, c)).start()
+            return carry
+        lax.fori_loop(1, 16, one, 0)
+        pltpu.make_async_copy(pair_ref.at[pl.ds(4 * col + 2 * part, 2)], pair_rows.at[col, rows], local.at[6 + part]).start()
+
     mask = mask_ref[...].astype(F32)
     pair_f[...] = pair_ref[...].astype(F32).reshape(2048, 128)
     pick_rows = one_hot((512, 128), lambda a, b: a == row * 64 + lax.rem(b, 64))
@@ -93,19 +103,20 @@
     lanes16 = lax.broadcasted_iota(jnp.int32, (16, 128), 1)
     pair_mask = jnp.where(lanes16 < 64, even, odd) * row_mask
     mul_in_t = mul_in_ref[...].T
-    for step in range(8):
-        if step == 4:
+    for step in range(2):
+        if step == 1:
             pl.semaphore_wait(barrier, 22)
             signal_row(ready)
-        parts = [pair_f[pl.ds(4 * step + u, 64, stride=32), :] for u in range(4)]
+            send_pair(0)
+        parts = [pair_f[pl.ds(16 * step + u, 64, stride=32), :] for u in range(16)]
         normed = norm(jnp.concatenate(parts, axis=0).T, 0)
         projected = dot(mul_in_t, normed)
-        masks = jnp.concatenate([pair_mask[2 * step : 2 * step + 1], pair_mask[2 * step + 1 : 2 * step + 2]], axis=1)
+        masks = jnp.concatenate([pair_mask[8 * step + v : 8 * step + v + 1] for v in range(8)], axis=1)
         left = masks * jax.nn.sigmoid(projected[128:256]) * projected[:128]
         right = masks * jax.nn.sigmoid(projected[384:]) * projected[256:384]
-        for v in range(2):
-            lr_f[pl.ds(2 * step + v, 128, stride=32), :] = left[:, v * 128 : v * 128 + 128]
-            lr_f[pl.ds(16 + 2 * step + v, 128, stride=32), :] = right[:, v * 128 : v * 128 + 128]
+        for v in range(8):
+            lr_f[pl.ds(8 * step + v, 128, stride=32), :] = left[:, v * 128 : v * 128 + 128]
+            lr_f[pl.ds(16 + 8 * step + v, 128, stride=32), :] = right[:, v * 128 : v * 128 + 128]
     lr_s[...] = lr_f[...].reshape(128, 2, 16, 128).astype(BF16)
 
     for one in loads[3:]:
@@ -145,39 +156,38 @@
 
     all_here(lr_s, lr_r, 0)
 
-    def send_pair(s, carry):
-        c = lax.rem(col + s, 16)
-        remote(pair_ref.at[pl.ds(4 * c, 4)], pair_rows.at[col], 1, (row, c)).start()
-        return carry
-    lax.fori_loop(1, 16, send_pair, 0)
-    pltpu.make_async_copy(pair_ref.at[pl.ds(4 * col, 4)], pair_rows.at[col], local.at[1]).start()
-
+    send_pair(1)
     for side, at in ((0, at_l), (1, at_r)):
+        here = [
+            jnp.concatenate([lr_r[(2 * rp + o) * 16 : (2 * rp + o + 1) * 16, side].reshape(256, 128) for o in range(2)], axis=1)
+            for rp in range(4)
+        ]
+        turned = dot(jnp.concatenate(here, axis=0), orders[side]).astype(BF16)
         for rp in range(4):
-            here = [lr_r[(2 * rp + o) * 16 : (2 * rp + o + 1) * 16, side].reshape(256, 128) for o in range(2)]
-            turned = dot(jnp.concatenate(here, axis=1), orders[side]).astype(BF16)
-            at[0:256, rp * 128 : rp * 128 + 128] = turned[:, :128]
-            at[256:512, rp * 128 : rp * 128 + 128] = turned[:, 128:]
+            for k in range(2):
+                at[k * 256 : k * 256 + 256, rp * 128 : rp * 128 + 128] = turned[rp * 256 : rp * 256 + 256, k * 128 : k * 128 + 128]
+    product = dot(at_l[...], at_r[...], 0, 0)
     for rp in range(4):
-        product = dot(at_l[:, rp * 128 : rp * 128 + 128].T, at_r[...])
         for il in range(4):
+            at = rp * 128 + il * 32
             for jt in range(4):
-                m_f[pl.ds(rp * 512 + il * 4 + jt, 32, stride=16), :] = product[il * 32 : il * 32 + 32, jt * 128 : jt * 128 + 128]
+                m_f[pl.ds(rp * 512 + il * 4 + jt, 32, stride=16), :] = product[at : at + 32, jt * 128 : jt * 128 + 128]
     m_s[...] = m_f[...].reshape(128, 16, 128).astype(BF16)
     to_all(m_s, m_r, 2)
 
-    pltpu.make_async_copy(pair_ref.at[pl.ds(0, 4)], pair_rows.at[0], local.at[1]).wait()
-    whole = remote(pair_rows.at[pl.ds(0, 15)], pair_rows.at[pl.ds(0, 15)], 1, (row, col))
-    whole.wait_send()
-    whole.wait_recv()
-
-    def pair_tile(jt, il):
-        return pair_rows[4 * jt : 4 * jt + 4, il].reshape(128, 128).astype(F32)
-
-    for jt in range(4):
-        for il in range(4):
-            at = (il * 4 + jt) * 128
-            pair_f[at : at + 128] = jax.nn.sigmoid(dot(norm(pair_tile(jt, il), 1), mul_gate_ref[...]))
+    for part in range(2):
+        rows = pl.ds(2 * part, 2)
+        pltpu.make_async_copy(pair_ref.at[pl.ds(0, 2)], pair_rows.at[0, rows], local.at[6 + part]).wait()
+        whole = remote(pair_rows.at[pl.ds(0, 15), rows], pair_rows.at[pl.ds(0, 15), rows], 6 + part, (row, col))
+        whole.wait_send()
+        whole.wait_recv()
+
+    def pair_block(half):
+        blocks = [pair_rows[8 * half : 8 * half + 8, il].reshape(256, 128) for il in range(4)]
+        return jnp.concatenate(blocks, axis=0).astype(F32)
+
+    for half in range(2):
+        pair_f[half * 1024 : half * 1024 + 1024] = jax.nn.sigmoid(dot(norm(pair_block(half), 1), mul_gate_ref[...]))
     all_here(m_s, m_r, 2)
 
     def slab(o, phase, full):
@@ -188,7 +198,7 @@
             return biases[o].at[c, pl.ds(0, 3)] if full else biases[o].at[c, b]
         return biases[o].at[pl.ds(0, 3)] if full else biases[o].at[c]
 
-    early, late = (0, 1, 2), (3, 4)
+    early, late = (0, 1, 2), (3, 4, 5)
 
     def gather_start(phase, which):
         for s in (1, 3, 2):
@@ -212,19 +222,22 @@
 
     m_f[...] = m_r[...].astype(F32).reshape(2048, 128)
     bias_in = jnp.concatenate([att_bias_ref[...].astype(F32), jnp.zeros((4, 128), F32)], axis=0).astype(BF16)
-    for jt in range(4):
+    for half in range(2):
+        tiles = [m_f[pl.ds(il * 4 + 2 * half + t, 128, stride=16), :] for il in range(4) for t in range(2)]
+        update = dot(norm(jnp.concatenate(tiles, axis=1), 0), mul_out_ref[...], 0, 0)
+        one = (pair_block(half) + pair_f[half * 1024 : half * 1024 + 1024] * update).astype(BF16)
+        normed = norm(one.astype(F32), 1)
+        bias = dot(bias_in, normed, 1, 1)
         for il in range(4):
-            at = il * 4 + jt
-            mix = norm(m_f[pl.ds(at, 128, stride=16), :], 0)
-            update = dot(mix, mul_out_ref[...], 0, 0)
-            one = (pair_tile(jt, il) + pair_f[at * 128 : at * 128 + 128] * update).astype(BF16)
-            one_all[core * 4 + il, jt * 128 : jt * 128 + 128] = one
-            bias = dot(bias_in, norm(one.astype(F32), 1), 1, 1)
-            for h in range(4):
-                o, slot = (jt, h // 2) if jt < 3 else (3 + h // 2, 0)
-                a, b, c = (place[axis] for axis in ORDERS[o])
-                biases[o][c, b, a, slot, h % 2 * 4 + il : h % 2 * 4 + il + 1, :] = bias[h : h + 1]
-        if jt == 2:
+            one_all[core * 4 + il, half * 256 : half * 256 + 256] = one[il * 256 : il * 256 + 256]
+            normed_all[il, half * 256 : half * 256 + 256] = normed[il * 256 : il * 256 + 256]
+            for t in range(2):
+                lanes = slice((il * 2 + t) * 128, (il * 2 + t) * 128 + 128)
+                for h in range(4):
+                    o, slot = WHERE[h // 2, 2 * half + t]
+                    a, b, c = (place[axis] for axis in ORDERS[o])
+                    biases[o][c, b, a, slot, h % 2 * 4 + il : h % 2 * 4 + il + 1, :] = bias[h : h + 1, lanes]
+        if half == 0:
             gather_start(0, early)
     gather_start(0, late)
     sibling = (row, col + 1 - 2 * core)
@@ -233,49 +246,42 @@
 
     heads = lax.broadcasted_iota(jnp.int32, (256, 128), 1) // 32
 
-    def project(i):
-        one = one_all[i]
-        normed = norm(one.astype(F32), 1)
-        normed_mine = dot(mine, normed).astype(BF16)
-        one_mine[i] = dot(mine, one)
+    def project(first, normed):
+        four = pl.ds(first, 4)
         kv = dot(normed, att_in_ref[:, 128:384]).astype(BF16)
-        keys[i] = kv[:, :128]
-        values[i] = kv[:, 128:]
-        query = dot(normed_mine, att_in_ref[:, :128])
-        for h in range(4):
-            queries[i, h * 256 : h * 256 + 256] = jnp.where(heads == h, query, 0.0).astype(BF16)
-        gates[i] = jax.nn.sigmoid(dot(normed_mine, att_in_ref[:, 384:]))
-
-    def project_own(n, carry):
-        project(core * 4 + n)
-        return carry
-
-    def project_other(n, carry):
-        project(4 - core * 4 + n)
-        return carry
-
-    lax.fori_loop(0, 2, project_own, 0)
+        keys[four] = kv[:, :128].reshape(4, 512, 128)
+        values[four] = kv[:, 128:].reshape(4, 512, 128)
+        picked = []
+        for n in range(4):
+            both = dot(mine, jnp.concatenate([normed[n * 512 : n * 512 + 512], one_all[first + n]], axis=1))
+            picked.append(both[:, :128].astype(BF16))
+            one_mine[first + n] = both[:, 128:]
+        picked = jnp.concatenate(picked, axis=0)
+        query = dot(picked, att_in_ref[:, :128])
+        for n in range(4):
+            for h in range(4):
+                queries[first + n, h * 256 : h * 256 + 256] = jnp.where(heads == h, query[n * 256 : n * 256 + 256], 0.0).astype(BF16)
+        gates[four] = jax.nn.sigmoid(dot(picked, att_in_ref[:, 384:])).reshape(4, 256, 128)
+
+    project(core * 4, normed_all[...].reshape(2048, 128))
     for group in (early, late):
         gather_wait(0, group)
         gather_start(1, group)
-    lax.fori_loop(2, 4, project_own, 0)
+    swap.wait()
+    other = 4 - core * 4
+    project(other, norm(one_all[pl.ds(other, 4)].reshape(2048, 128).astype(F32), 1))
     for group in (early, late):
         gather_wait(1, group)
         gather_start(2, group)
-    swap.wait()
-    lax.fori_loop(0, 4, project_other, 0)
-    gather_wait(2, early)
-    gather_wait(2, late)
 
     mask_term = 1000000000.0 * (mask - 1.0)
     upper = lax.broadcasted_iota(jnp.int32, (8, 128), 0) < 4
 
-    def build(n, carry):
+    def build(half, n, carry):
         x, y = lax.rem(n // 2, 4), lax.rem(n, 2) * 2 + n // 8
-        for u in range(8):
-            hp, kt = u // 4, u % 4
-            o, slot = (kt, hp) if kt < 3 else (3 + hp, 0)
-            lanes = pl.ds(u % 4 * 128, 128)
+        for hp, kt in ((0, 2 * half), (1, 2 * half), (0, 2 * half + 1), (1, 2 * half + 1)):
+            o, slot = WHERE[hp, kt]
+            lanes = pl.ds(kt * 128, 128)
             for zp in range(2):
                 tiles = []
                 for z in (2 * zp, 2 * zp + 1):
@@ -289,12 +295,14 @@
                     jnp.where(upper, pltpu.roll(tiles[0], 4, 0), tiles[1]),
                 )
                 for h2 in range(2):
-                    h = u // 4 * 2 + h2
-                    value = mixed[h2] + chain_bias_ref[0, h] * together + mask_term[:, u % 4 * 128 : u % 4 * 128 + 128]
+                    h = hp * 2 + h2
+                    value = mixed[h2] + chain_bias_ref[0, h] * together + mask_term[:, kt * 128 : kt * 128 + 128]
                     table[h, rows, lanes] = value * LOG2E
         return carry
 
-    lax.fori_loop(0, 16, build, 0)
+    for half, group in enumerate((early, late)):
+        gather_wait(2, group)
+        lax.fori_loop(0, 16, functools.partial(build, half), 0)
 
     scale = 32 ** (-0.5) * LOG2E
 
@@ -306,24 +314,24 @@
             rows = slice(n * 64, n * 64 + 64)
             scores = score_s[slot, rows] * scale + table[n // 4, n % 4 * 64 : n % 4 * 64 + 64]
             weights = jnp.exp2(scores - jnp.max(scores, axis=1, keepdims=True))
-            total_s[slot, rows] = jnp.broadcast_to(jnp.sum(weights, axis=1, keepdims=True), (64, 128))
+            total_s[slot, rows] = jnp.broadcast_to(1.0 / jnp.sum(weights, axis=1, keepdims=True), (64, 128))
             weight_s[slot, rows] = weights.astype(BF16)
 
-    def finish(i, slot):
-        weighted = dot(weight_s[slot], values[i]) / total_s[slot]
+    def attend(i, slot):
+        weighted = dot(weight_s[slot], values[i]) * total_s[slot]
         total = jnp.zeros((256, 128), F32)
         for h in range(4):
             total = total + jnp.where(heads == h, weighted[h * 256 : h * 256 + 256], 0.0)
-        gated = (gates[i] * total).astype(BF16)
-        two = (one_mine[i] + dot(gated, att_out_ref[...])).astype(BF16)
+        gated_s[i] = (gates[i] * total).astype(BF16)
+
+    def finish(part):
+        rows = pl.ds(part * 4, 4)
+        two = (one_mine[rows].reshape(1024, 128) + dot(gated_s[rows].reshape(1024, 128), att_out_ref[...])).astype(BF16)
         two_f = two.astype(F32)
         inner = jnp.maximum(dot(norm(two_f, 1), up_ref[...]), 0.0).astype(BF16)
-        result = (two_f + dot(inner, down_ref[...])).astype(BF16)
-        out_s[:, i] = result.reshape(16, 16, 128)
-
-    def send_out(part):
-        first, count = OUT_ROWS[part]
-        rows = pl.ds(first, count)
+        result = (two_f + dot(inner, down_ref[...])).astype(BF16).reshape(4, 16, 16, 128)
+        for n in range(4):
+            out_s[:, part * 4 + n] = result[n]
 
         def one(s, carry):
             c = lax.rem(col + s, 16)
@@ -336,16 +344,15 @@
     for i in range(8):
         if i < 7:
             score(i + 1, (i + 1) % 2)
+        if i > 0:
+            attend(i - 1, (i - 1) % 2)
+        if i == 4:
+            finish(0)
         soften(i % 2)
-        if i > 0:
-            finish(i - 1, (i - 1) % 2)
-        for part in range(2):
-            if i == OUT_ROWS[part + 1][0]:
-                send_out(part)
-    finish(7, 1)
-    send_out(2)
-    for part in range(3):
-        rows = pl.ds(*OUT_ROWS[part])
+    attend(7, 1)
+    finish(1)
+    for part in range(2):
+        rows = pl.ds(part * 4, 4)
         pltpu.make_async_copy(out_s.at[col, rows], out_r.at[col, rows], local.at[4 + part]).wait()
         whole = remote(out_s.at[pl.ds(0, 15), rows], out_r.at[pl.ds(0, 15), rows], 4 + part, (row, col))
         whole.wait_send()
@@ -356,9 +363,10 @@
         return b == which * 128 + il * 16 + group * 4 + jl
 
     back = one_hot((256, 256), place_out)
+    blocks = jnp.concatenate([out_r[2 * chip : 2 * chip + 2].reshape(256, 128) for chip in range(8)], axis=1)
+    placed = dot(back, blocks).astype(BF16)
     for chip in range(8):
-        block = out_r[2 * chip : 2 * chip + 2].reshape(256, 128)
-        out_ref[8 * chip : 8 * chip + 8] = dot(back, block).astype(BF16).reshape(8, 32, 128)
+        out_ref[8 * chip : 8 * chip + 8] = placed[:, chip * 128 : chip * 128 + 128].reshape(8, 32, 128)
 
 
 def body(pair_rep, residue_mask, chain_index, mul_in, mul_gate, mul_out, att_in, att_bias, chain_bias, att_out, trans_up, trans_down):
@@ -388,8 +396,10 @@
             pltpu.VMEM((128, 16, 128), BF16),
             pltpu.VMEM((16, 4, 32, 128), BF16),
             pltpu.VMEM((8, 512, 128), BF16),
+            pltpu.VMEM((4, 512, 128), BF16),
             pltpu.VMEM((4, 4, 4, 2, 8, 128), F32),
-            pltpu.VMEM((4, 4, 4, 2, 8, 128), F32),
+            pltpu.VMEM((4, 4, 4, 1, 8, 128), F32),
+            pltpu.VMEM((4, 4, 4, 1, 8, 128), F32),
             pltpu.VMEM((4, 4, 4, 2, 8, 128), F32),
             pltpu.VMEM((4, 4, 4, 1, 8, 128), F32),
             pltpu.VMEM((4, 4, 4, 1, 8, 128), F32),
@@ -403,15 +413,16 @@
             pltpu.VMEM((2, 1024, 512), F32),
             pltpu.VMEM((2, 1024, 512), BF16),
             pltpu.VMEM((2, 1024, 128), F32),
+            pltpu.VMEM((8, 256, 128), BF16),
             pltpu.VMEM((16, 8, 16, 128), BF16),
             pltpu.VMEM((16, 8, 16, 128), BF16),
             sem.REGULAR,
             sem.DMA((11,)),
-            sem.DMA((7,)),
-            sem.DMA((7,)),
-            sem.DMA((7,)),
-            sem.DMA((5, 3)),
-            sem.DMA((5, 3)),
+            sem.DMA((8,)),
+            sem.DMA((8,)),
+            sem.DMA((8,)),
+            sem.DMA((6, 3)),
+            sem.DMA((6, 3)),
         ],
         compiler_params=pltpu.CompilerParams(collective_id=0, has_side_effects=True, vmem_limit_bytes=56 * 1024 * 1024),
     )(*args)

time: 87.8 us -> 76.5 us (0.87)
  Pallas kernels: 85.7 us -> 74.4 us
    pallas_call x1, Pallas kernels: 85.7 us -> 74.4 us  [body(): pl.pallas_call(kernel, out_shape=jax.ShapeDtypeStruct(pair_rep.shape, BF1...]
where the time goes in v3:
time: 76.5 us; the launch traced here: 76.3 us
  Pallas kernels  74.4 us (97%)
  local copies, waits for them, and re-layouts  1.87 us (2%)
    pallas_call x1, Pallas kernels, body(): pl.pallas_call(kernel, out_shape=jax.ShapeDtypeStruct(pair_rep.shape, BF1...  74.4 us
    unnamed x1, local copies, waits for them, and re-layouts  1.87 us

profile of v3, /device:TPU:1, one launch (start us, length us, event | category | flops | bytes accessed | tf_op | source)
XLA Modules:
  0.0 76.3 jit_solution(11933967015291058171)
XLA Ops:
  0.0 74.4 %shard_map.118 = bf16[64,32,128]{2,1,0:T(8,128)(2,1)} custom-call(bf16[64,32,128]{2,1,0:T(8,128)(2,1)} %pair_in.1, s32[1,512]{1,0:T(1,128)} %bitcast.4, s32[1,512]{1,0:T(1,128)} %bitcast.5, bf16[128,512]{1,0:T(8,128)(2,1)} %mul_in_in.1, bf16[128,128]{1,0:T(8,128)(2,1)} %mul_gate_in.1, bf16[128,128]{1,0:T(8,128)(2,1)} %mul_out_in.1, ...), custom_call_target="tpu_custom_call" | custom-call | tf_op jit(solution)/shard_map/pallas_call | solution.py:381
  74.4 1.9 %copy.14 = bf16[64,32,128]{2,1,0:T(8,128)(2,1)} copy(bf16[64,32,128]{2,1,0:T(8,128)(2,1)} %shard_map.118) | data formatting | bytes 1048576

commit v4 on v3

--- a/solution.py
+++ b/solution.py
@@ -14,7 +14,7 @@
 EPS = 1e-05
 LOG2E = math.log2(math.e)
 ORDERS = ((0, 1, 2), (1, 2, 0), (2, 0, 1), (1, 2, 0), (0, 1, 2), (2, 0, 1))
-WHERE = {(0, 0): (0, 0), (1, 0): (0, 1), (0, 1): (1, 0), (1, 1): (2, 0), (0, 2): (3, 0), (1, 2): (3, 1), (0, 3): (4, 0), (1, 3): (5, 0)}
+WHERE = {(0, 0): (0, 0), (0, 1): (0, 1), (0, 2): (1, 0), (0, 3): (2, 0), (1, 0): (3, 0), (1, 1): (3, 1), (1, 2): (4, 0), (1, 3): (5, 0)}
 
 
 def norm(values, axis):
@@ -80,8 +80,7 @@
     signal_col(barrier)
     for one in loads[3:]:
         one.start()
-    for one in loads[:3]:
-        one.wait()
+    loads[0].wait()
 
     def send_pair(part):
         rows = pl.ds(2 * part, 2)
@@ -94,7 +93,6 @@
         pltpu.make_async_copy(pair_ref.at[pl.ds(4 * col + 2 * part, 2)], pair_rows.at[col, rows], local.at[6 + part]).start()
 
     mask = mask_ref[...].astype(F32)
-    pair_f[...] = pair_ref[...].astype(F32).reshape(2048, 128)
     pick_rows = one_hot((512, 128), lambda a, b: a == row * 64 + lax.rem(b, 64))
     row_mask = dot(jnp.broadcast_to(mask, (16, 512)).astype(BF16), pick_rows)
     place_col = lax.broadcasted_iota(jnp.int32, (16, 512), 1) - (col * 32 + 2 * lax.broadcasted_iota(jnp.int32, (16, 512), 0))
@@ -102,11 +100,15 @@
     odd = jnp.sum(jnp.where(place_col == 1, mask, 0.0), axis=1, keepdims=True)
     lanes16 = lax.broadcasted_iota(jnp.int32, (16, 128), 1)
     pair_mask = jnp.where(lanes16 < 64, even, odd) * row_mask
+    loads[1].wait()
+    loads[2].wait()
+    pair_f[...] = pair_ref[...].astype(F32).reshape(2048, 128)
     mul_in_t = mul_in_ref[...].T
     for step in range(2):
         if step == 1:
             pl.semaphore_wait(barrier, 22)
-            signal_row(ready)
+            for s in range(1, 8):
+                pl.semaphore_signal(ready.at[s], inc=1, device_id=(lax.rem(row + s, 8), col), device_id_type=MESH)
             send_pair(0)
         parts = [pair_f[pl.ds(16 * step + u, 64, stride=32), :] for u in range(16)]
         normed = norm(jnp.concatenate(parts, axis=0).T, 0)
@@ -121,14 +123,21 @@
 
     for one in loads[3:]:
         one.wait()
-    pl.semaphore_wait(ready, 7)
+
+    def to_row(src, dst, which, s):
+        r = lax.rem(row + s, 8)
+
+        def one(n, carry):
+            c = lax.rem(col + n, 16)
+            remote(src.at[r * 16 + c], dst.at[me], which, (r, c)).start()
+            return carry
+        lax.fori_loop(1 if s == 0 else 0, 16, one, 0)
 
     def to_all(src, dst, which):
-        def one(s, carry):
-            r, c = lax.rem(row + s // 16, 8), lax.rem(col + lax.rem(s, 16), 16)
-            remote(src.at[r * 16 + c], dst.at[me], which, (r, c)).start()
-            return carry
-        lax.fori_loop(1, 128, one, 0)
+        for s in range(8):
+            if s > 0 and which == 0:
+                pl.semaphore_wait(ready.at[8 - s], 1)
+            to_row(src, dst, which, s)
         pltpu.make_async_copy(src.at[me], dst.at[me], local.at[which]).start()
 
     def all_here(src, dst, which):
@@ -190,32 +199,47 @@
         pair_f[half * 1024 : half * 1024 + 1024] = jax.nn.sigmoid(dot(norm(pair_block(half), 1), mul_gate_ref[...]))
     all_here(m_s, m_r, 2)
 
-    def slab(o, phase, full):
-        a, b, c = (place[axis] for axis in ORDERS[o])
-        if phase == 0:
-            return biases[o].at[c, b, pl.ds(0, 3)] if full else biases[o].at[c, b, a]
-        if phase == 1:
-            return biases[o].at[c, pl.ds(0, 3)] if full else biases[o].at[c, b]
-        return biases[o].at[pl.ds(0, 3)] if full else biases[o].at[c]
-
     early, late = (0, 1, 2), (3, 4, 5)
 
-    def gather_start(phase, which):
+    def plane_start(which):
+        def one(n, carry):
+            for o in which:
+                a, b, c = ORDERS[o]
+                there = list(place)
+                there[a] = lax.rem(place[a] + lax.rem(n, 4), 4)
+                there[b] = lax.rem(place[b] + n // 4, 4)
+                ref = biases[o].at[place[c], place[b], place[a]]
+                pltpu.make_async_remote_copy(
+                    ref, ref, gather_send.at[o, 0], gather_recv.at[o, 0], device_id=device_at(there), device_id_type=MESH
+                ).start()
+            return carry
+        lax.fori_loop(1, 16, one, 0)
+
+    def plane_wait(which):
+        for o in which:
+            ref = m_f.at[pl.ds(0, 120 * biases[o].shape[3])]
+            whole = pltpu.make_async_remote_copy(
+                ref, ref, gather_send.at[o, 0], gather_recv.at[o, 0], device_id=(row, col), device_id_type=MESH
+            )
+            whole.wait_send()
+            whole.wait_recv()
+
+    def axis_start(which):
         for s in (1, 3, 2):
             for o in which:
-                axis = ORDERS[o][phase]
+                c = ORDERS[o][2]
                 there = list(place)
-                there[axis] = lax.rem(place[axis] + s, 4)
-                ref = slab(o, phase, False)
+                there[c] = lax.rem(place[c] + s, 4)
+                ref = biases[o].at[place[c]]
                 pltpu.make_async_remote_copy(
-                    ref, ref, gather_send.at[o, phase], gather_recv.at[o, phase], device_id=device_at(there), device_id_type=MESH
+                    ref, ref, gather_send.at[o, 1], gather_recv.at[o, 1], device_id=device_at(there), device_id_type=MESH
                 ).start()
 
-    def gather_wait(phase, which):
+    def axis_wait(which):
         for o in which:
-            ref = slab(o, phase, True)
+            ref = biases[o].at[pl.ds(0, 3)]
             whole = pltpu.make_async_remote_copy(
-                ref, ref, gather_send.at[o, phase], gather_recv.at[o, phase], device_id=(row, col), device_id_type=MESH
+                ref, ref, gather_send.at[o, 1], gather_recv.at[o, 1], device_id=(row, col), device_id_type=MESH
             )
             whole.wait_send()
             whole.wait_recv()
@@ -237,9 +261,8 @@
                     o, slot = WHERE[h // 2, 2 * half + t]
                     a, b, c = (place[axis] for axis in ORDERS[o])
                     biases[o][c, b, a, slot, h % 2 * 4 + il : h % 2 * 4 + il + 1, :] = bias[h : h + 1, lanes]
-        if half == 0:
-            gather_start(0, early)
-    gather_start(0, late)
+    plane_start(early)
+    plane_start(late)
     sibling = (row, col + 1 - 2 * core)
     swap = remote(one_all.at[pl.ds(core * 4, 4)], one_all.at[pl.ds(core * 4, 4)], 3, sibling)
     swap.start()
@@ -263,23 +286,21 @@
                 queries[first + n, h * 256 : h * 256 + 256] = jnp.where(heads == h, query[n * 256 : n * 256 + 256], 0.0).astype(BF16)
         gates[four] = jax.nn.sigmoid(dot(picked, att_in_ref[:, 384:])).reshape(4, 256, 128)
 
+    plane_wait(early)
+    axis_start(early)
     project(core * 4, normed_all[...].reshape(2048, 128))
-    for group in (early, late):
-        gather_wait(0, group)
-        gather_start(1, group)
+    plane_wait(late)
+    axis_start(late)
     swap.wait()
     other = 4 - core * 4
     project(other, norm(one_all[pl.ds(other, 4)].reshape(2048, 128).astype(F32), 1))
-    for group in (early, late):
-        gather_wait(1, group)
-        gather_start(2, group)
 
     mask_term = 1000000000.0 * (mask - 1.0)
     upper = lax.broadcasted_iota(jnp.int32, (8, 128), 0) < 4
 
-    def build(half, n, carry):
+    def build(hp, n, carry):
         x, y = lax.rem(n // 2, 4), lax.rem(n, 2) * 2 + n // 8
-        for hp, kt in ((0, 2 * half), (1, 2 * half), (0, 2 * half + 1), (1, 2 * half + 1)):
+        for kt in range(4):
             o, slot = WHERE[hp, kt]
             lanes = pl.ds(kt * 128, 128)
             for zp in range(2):
@@ -300,29 +321,24 @@
                     table[h, rows, lanes] = value * LOG2E
         return carry
 
-    for half, group in enumerate((early, late)):
-        gather_wait(2, group)
-        lax.fori_loop(0, 16, functools.partial(build, half), 0)
-
     scale = 32 ** (-0.5) * LOG2E
 
-    def score(i, slot):
-        score_s[slot] = dot(queries[i], keys[i], 1, 1)
-
-    def soften(slot):
-        for n in range(16):
+    def score(hp, i, slot):
+        score_s[slot] = dot(queries[i, hp * 512 : hp * 512 + 512], keys[i], 1, 1)
+
+    def soften(hp, slot):
+        for n in range(8):
             rows = slice(n * 64, n * 64 + 64)
-            scores = score_s[slot, rows] * scale + table[n // 4, n % 4 * 64 : n % 4 * 64 + 64]
+            scores = score_s[slot, rows] * scale + table[2 * hp + n // 4, n % 4 * 64 : n % 4 * 64 + 64]
             weights = jnp.exp2(scores - jnp.max(scores, axis=1, keepdims=True))
             total_s[slot, rows] = jnp.broadcast_to(1.0 / jnp.sum(weights, axis=1, keepdims=True), (64, 128))
             weight_s[slot, rows] = weights.astype(BF16)
 
-    def attend(i, slot):
+    def attend(hp, i, slot):
         weighted = dot(weight_s[slot], values[i]) * total_s[slot]
-        total = jnp.zeros((256, 128), F32)
-        for h in range(4):
-            total = total + jnp.where(heads == h, weighted[h * 256 : h * 256 + 256], 0.0)
-        gated_s[i] = (gates[i] * total).astype(BF16)
+        total = jnp.where(heads == 2 * hp, weighted[:256], jnp.where(heads == 2 * hp + 1, weighted[256:], 0.0))
+        gated = (gates[i] * total).astype(BF16)
+        gated_s[i] = gated if hp == 0 else jnp.where(heads < 2, gated_s[i], gated)
 
     def finish(part):
         rows = pl.ds(part * 4, 4)
@@ -333,6 +349,9 @@
         for n in range(4):
             out_s[:, part * 4 + n] = result[n]
 
+    def send_out(part):
+        rows = pl.ds(part * 4, 4)
+
         def one(s, carry):
             c = lax.rem(col + s, 16)
             remote(out_s.at[c, rows], out_r.at[col, rows], 4 + part, (row, c)).start()
@@ -340,17 +359,23 @@
         lax.fori_loop(1, 16, one, 0)
         pltpu.make_async_copy(out_s.at[col, rows], out_r.at[col, rows], local.at[4 + part]).start()
 
-    score(0, 0)
-    for i in range(8):
-        if i < 7:
-            score(i + 1, (i + 1) % 2)
-        if i > 0:
-            attend(i - 1, (i - 1) % 2)
-        if i == 4:
-            finish(0)
-        soften(i % 2)
-    attend(7, 1)
+    for hp, group in enumerate((early, late)):
+        score(hp, 0, 0)
+        axis_wait(group)
+        lax.fori_loop(0, 16, functools.partial(build, hp), 0)
+        for i in range(8):
+            if i < 7:
+                score(hp, i + 1, (i + 1) % 2)
+            if i > 0:
+                attend(hp, i - 1, (i - 1) % 2)
+            if hp == 1 and i == 4:
+                finish(0)
+            soften(hp, i % 2)
+            if hp == 1 and i == 4:
+                send_out(0)
+        attend(hp, 7, 1)
     finish(1)
+    send_out(1)
     for part in range(2):
         rows = pl.ds(part * 4, 4)
         pltpu.make_async_copy(out_s.at[col, rows], out_r.at[col, rows], local.at[4 + part]).wait()
@@ -410,19 +435,19 @@
             pltpu.VMEM((8, 1024, 128), BF16),
             pltpu.VMEM((8, 256, 128), F32),
             pltpu.VMEM((8, 256, 128), F32),
-            pltpu.VMEM((2, 1024, 512), F32),
-            pltpu.VMEM((2, 1024, 512), BF16),
-            pltpu.VMEM((2, 1024, 128), F32),
+            pltpu.VMEM((2, 512, 512), F32),
+            pltpu.VMEM((2, 512, 512), BF16),
+            pltpu.VMEM((2, 512, 128), F32),
             pltpu.VMEM((8, 256, 128), BF16),
             pltpu.VMEM((16, 8, 16, 128), BF16),
             pltpu.VMEM((16, 8, 16, 128), BF16),
-            sem.REGULAR,
+            sem.REGULAR((8,)),
             sem.DMA((11,)),
             sem.DMA((8,)),
             sem.DMA((8,)),
             sem.DMA((8,)),
-            sem.DMA((6, 3)),
-            sem.DMA((6, 3)),
+            sem.DMA((6, 2)),
+            sem.DMA((6, 2)),
         ],
         compiler_params=pltpu.CompilerParams(collective_id=0, has_side_effects=True, vmem_limit_bytes=56 * 1024 * 1024),
     )(*args)

time: 76.5 us -> 74.3 us (0.971)
  Pallas kernels: 74.4 us -> 72.2 us
    pallas_call x1, Pallas kernels: 74.4 us -> 72.2 us  [body(): pl.pallas_call(kernel, out_shape=jax.ShapeDtypeStruct(pair_rep.shape, BF1...]
where the time goes in v4:
time: 74.3 us; the launch traced here: 74.1 us
  Pallas kernels  72.2 us (97%)
  local copies, waits for them, and re-layouts  1.87 us (3%)
    pallas_call x1, Pallas kernels, body(): pl.pallas_call(kernel, out_shape=jax.ShapeDtypeStruct(pair_rep.shape, BF1...  72.2 us
    unnamed x1, local copies, waits for them, and re-layouts  1.87 us

profile of v4, /device:TPU:1, one launch (start us, length us, event | category | flops | bytes accessed | tf_op | source)
XLA Modules:
  0.0 74.1 jit_solution(18199894406133687809)
XLA Ops:
  0.0 72.2 %shard_map.118 = bf16[64,32,128]{2,1,0:T(8,128)(2,1)} custom-call(bf16[64,32,128]{2,1,0:T(8,128)(2,1)} %pair_in.1, s32[1,512]{1,0:T(1,128)} %bitcast.4, s32[1,512]{1,0:T(1,128)} %bitcast.5, bf16[128,512]{1,0:T(8,128)(2,1)} %mul_in_in.1, bf16[128,128]{1,0:T(8,128)(2,1)} %mul_gate_in.1, bf16[128,128]{1,0:T(8,128)(2,1)} %mul_out_in.1, ...), custom_call_target="tpu_custom_call" | custom-call | tf_op jit(solution)/shard_map/pallas_call | solution.py:406
  72.2 1.9 %copy.14 = bf16[64,32,128]{2,1,0:T(8,128)(2,1)} copy(bf16[64,32,128]{2,1,0:T(8,128)(2,1)} %shard_map.118) | data formatting | bytes 1048576

commit v5 on v4

--- a/solution.py
+++ b/solution.py
@@ -38,7 +38,7 @@
     att_out_in, up_in, down_in, out_ref,
     pair_ref, mask_ref, chain_ref, mul_in_ref, mul_gate_ref, mul_out_ref, att_in_ref, att_bias_ref, att_out_ref, up_ref, down_ref,
     pair_f, lr_f, lr_s, lr_r, at_l, at_r, m_f, m_s, m_r, pair_rows, one_all, normed_all, bias0, bias1, bias2, bias3, bias4, bias5, table, same,
-    keys, values, queries, gates, one_mine, score_s, weight_s, total_s, gated_s, out_s, out_r,
+    keys, values, queries, gates, one_mine, score_s, weight_s, gated_s, out_s, out_r,
     ready, load, local, send, recv, gather_send, gather_recv,
 ):
     row, col = lax.axis_index("row"), lax.axis_index("col")
@@ -269,18 +269,21 @@
 
     heads = lax.broadcasted_iota(jnp.int32, (256, 128), 1) // 32
 
+    scale = 32 ** (-0.5) * LOG2E
+
     def project(first, normed):
         four = pl.ds(first, 4)
         kv = dot(normed, att_in_ref[:, 128:384]).astype(BF16)
         keys[four] = kv[:, :128].reshape(4, 512, 128)
-        values[four] = kv[:, 128:].reshape(4, 512, 128)
+        values[four, :, 0:128] = kv[:, 128:].reshape(4, 512, 128)
+        values[four, :, 128:256] = jnp.ones((4, 512, 128), BF16)
         picked = []
         for n in range(4):
             both = dot(mine, jnp.concatenate([normed[n * 512 : n * 512 + 512], one_all[first + n]], axis=1))
             picked.append(both[:, :128].astype(BF16))
             one_mine[first + n] = both[:, 128:]
         picked = jnp.concatenate(picked, axis=0)
-        query = dot(picked, att_in_ref[:, :128])
+        query = dot(picked, att_in_ref[:, :128]) * scale
         for n in range(4):
             for h in range(4):
                 queries[first + n, h * 256 : h * 256 + 256] = jnp.where(heads == h, query[n * 256 : n * 256 + 256], 0.0).astype(BF16)
@@ -321,21 +324,20 @@
                     table[h, rows, lanes] = value * LOG2E
         return carry
 
-    scale = 32 ** (-0.5) * LOG2E
-
-    def score(hp, i, slot):
-        score_s[slot] = dot(queries[i, hp * 512 : hp * 512 + 512], keys[i], 1, 1)
-
-    def soften(hp, slot):
+
+    def score(hp, i):
+        score_s[hp, i] = dot(queries[i, hp * 512 : hp * 512 + 512], keys[i], 1, 1)
+
+    def soften(hp, i, slot):
         for n in range(8):
             rows = slice(n * 64, n * 64 + 64)
-            scores = score_s[slot, rows] * scale + table[2 * hp + n // 4, n % 4 * 64 : n % 4 * 64 + 64]
+            scores = score_s[hp, i, rows] + table[2 * hp + n // 4, n % 4 * 64 : n % 4 * 64 + 64]
             weights = jnp.exp2(scores - jnp.max(scores, axis=1, keepdims=True))
-            total_s[slot, rows] = jnp.broadcast_to(1.0 / jnp.sum(weights, axis=1, keepdims=True), (64, 128))
             weight_s[slot, rows] = weights.astype(BF16)
 
     def attend(hp, i, slot):
-        weighted = dot(weight_s[slot], values[i]) * total_s[slot]
+        weighted = dot(weight_s[slot], values[i])
+        weighted = weighted[:, :128] / weighted[:, 128:]
         total = jnp.where(heads == 2 * hp, weighted[:256], jnp.where(heads == 2 * hp + 1, weighted[256:], 0.0))
         gated = (gates[i] * total).astype(BF16)
         gated_s[i] = gated if hp == 0 else jnp.where(heads < 2, gated_s[i], gated)
@@ -359,18 +361,19 @@
         lax.fori_loop(1, 16, one, 0)
         pltpu.make_async_copy(out_s.at[col, rows], out_r.at[col, rows], local.at[4 + part]).start()
 
+    for i in range(8):
+        score(0, i)
     for hp, group in enumerate((early, late)):
-        score(hp, 0, 0)
         axis_wait(group)
         lax.fori_loop(0, 16, functools.partial(build, hp), 0)
         for i in range(8):
-            if i < 7:
-                score(hp, i + 1, (i + 1) % 2)
+            if hp == 0:
+                score(1, i)
             if i > 0:
                 attend(hp, i - 1, (i - 1) % 2)
             if hp == 1 and i == 4:
                 finish(0)
-            soften(hp, i % 2)
+            soften(hp, i, i % 2)
             if hp == 1 and i == 4:
                 send_out(0)
         attend(hp, 7, 1)
@@ -431,13 +434,12 @@
             pltpu.VMEM((4, 256, 512), F32),
             pltpu.VMEM((256, 512), F32),
             pltpu.VMEM((8, 512, 128), BF16),
-            pltpu.VMEM((8, 512, 128), BF16),
+            pltpu.VMEM((8, 512, 256), BF16),
             pltpu.VMEM((8, 1024, 128), BF16),
             pltpu.VMEM((8, 256, 128), F32),
             pltpu.VMEM((8, 256, 128), F32),
-            pltpu.VMEM((2, 512, 512), F32),
+            pltpu.VMEM((2, 8, 512, 512), F32),
             pltpu.VMEM((2, 512, 512), BF16),
-            pltpu.VMEM((2, 512, 128), F32),
             pltpu.VMEM((8, 256, 128), BF16),
             pltpu.VMEM((16, 8, 16, 128), BF16),
             pltpu.VMEM((16, 8, 16, 128), BF16),

time: 74.3 us -> 73 us (0.983)
  Pallas kernels: 72.2 us -> 70.9 us
    pallas_call x1, Pallas kernels: 72.2 us -> 70.9 us  [body(): pl.pallas_call(kernel, out_shape=jax.ShapeDtypeStruct(pair_rep.shape, BF1...]
where the time goes in v5:
time: 73 us; the launch traced here: 72.8 us
  Pallas kernels  70.9 us (97%)
  local copies, waits for them, and re-layouts  1.87 us (3%)
    pallas_call x1, Pallas kernels, body(): pl.pallas_call(kernel, out_shape=jax.ShapeDtypeStruct(pair_rep.shape, BF1...  70.9 us
    unnamed x1, local copies, waits for them, and re-layouts  1.87 us

profile of v5, /device:TPU:1, one launch (start us, length us, event | category | flops | bytes accessed | tf_op | source)
XLA Modules:
  0.0 72.8 jit_solution(11389090732724289421)
XLA Ops:
  0.0 70.9 %shard_map.118 = bf16[64,32,128]{2,1,0:T(8,128)(2,1)} custom-call(bf16[64,32,128]{2,1,0:T(8,128)(2,1)} %pair_in.1, s32[1,512]{1,0:T(1,128)} %bitcast.4, s32[1,512]{1,0:T(1,128)} %bitcast.5, bf16[128,512]{1,0:T(8,128)(2,1)} %mul_in_in.1, bf16[128,128]{1,0:T(8,128)(2,1)} %mul_gate_in.1, bf16[128,128]{1,0:T(8,128)(2,1)} %mul_out_in.1, ...), custom_call_target="tpu_custom_call" | custom-call | tf_op jit(solution)/shard_map/pallas_call | solution.py:409
  70.9 1.9 %copy.14 = bf16[64,32,128]{2,1,0:T(8,128)(2,1)} copy(bf16[64,32,128]{2,1,0:T(8,128)(2,1)} %shard_map.118) | data formatting | bytes 1048576

commit v6 on v5

--- a/solution.py
+++ b/solution.py
@@ -35,10 +35,10 @@
 
 def kernel(
     pair_in, mask_in, chain_in, mul_in_in, mul_gate_in, mul_out_in, att_in_in, att_bias_in, chain_bias_ref,
-    att_out_in, up_in, down_in, out_ref,
+    att_out_in, up_in, down_in, out_r,
     pair_ref, mask_ref, chain_ref, mul_in_ref, mul_gate_ref, mul_out_ref, att_in_ref, att_bias_ref, att_out_ref, up_ref, down_ref,
     pair_f, lr_f, lr_s, lr_r, at_l, at_r, m_f, m_s, m_r, pair_rows, one_all, normed_all, bias0, bias1, bias2, bias3, bias4, bias5, table, same,
-    keys, values, queries, gates, one_mine, score_s, weight_s, gated_s, out_s, out_r,
+    keys, values, queries, gates, one_mine, score_s, weight_s, gated_s, out_s,
     ready, load, local, send, recv, gather_send, gather_recv,
 ):
     row, col = lax.axis_index("row"), lax.axis_index("col")
@@ -261,7 +261,7 @@
                     o, slot = WHERE[h // 2, 2 * half + t]
                     a, b, c = (place[axis] for axis in ORDERS[o])
                     biases[o][c, b, a, slot, h % 2 * 4 + il : h % 2 * 4 + il + 1, :] = bias[h : h + 1, lanes]
-    plane_start(early)
+        plane_start((0,) if half == 0 else (1, 2))
     plane_start(late)
     sibling = (row, col + 1 - 2 * core)
     swap = remote(one_all.at[pl.ds(core * 4, 4)], one_all.at[pl.ds(core * 4, 4)], 3, sibling)
@@ -289,11 +289,13 @@
                 queries[first + n, h * 256 : h * 256 + 256] = jnp.where(heads == h, query[n * 256 : n * 256 + 256], 0.0).astype(BF16)
         gates[four] = jax.nn.sigmoid(dot(picked, att_in_ref[:, 384:])).reshape(4, 256, 128)
 
-    plane_wait(early)
-    axis_start(early)
+    for o in early:
+        plane_wait((o,))
+        axis_start((o,))
     project(core * 4, normed_all[...].reshape(2048, 128))
-    plane_wait(late)
-    axis_start(late)
+    for o in late:
+        plane_wait((o,))
+        axis_start((o,))
     swap.wait()
     other = 4 - core * 4
     project(other, norm(one_all[pl.ds(other, 4)].reshape(2048, 128).astype(F32), 1))
@@ -386,19 +388,8 @@
         whole.wait_send()
         whole.wait_recv()
 
-    def place_out(a, b):
-        il, group, which, jl = a // 32, lax.rem(a // 8, 4), lax.rem(a // 4, 2), lax.rem(a, 4)
-        return b == which * 128 + il * 16 + group * 4 + jl
-
-    back = one_hot((256, 256), place_out)
-    blocks = jnp.concatenate([out_r[2 * chip : 2 * chip + 2].reshape(256, 128) for chip in range(8)], axis=1)
-    placed = dot(back, blocks).astype(BF16)
-    for chip in range(8):
-        out_ref[8 * chip : 8 * chip + 8] = placed[:, chip * 128 : chip * 128 + 128].reshape(8, 32, 128)
-
 
 def body(pair_rep, residue_mask, chain_index, mul_in, mul_gate, mul_out, att_in, att_bias, chain_bias, att_out, trans_up, trans_down):
-    vmem = pl.BlockSpec(memory_space=pltpu.VMEM)
     specs = [pl.BlockSpec(memory_space=pl.ANY)] * 12
     specs[8] = pl.BlockSpec(memory_space=pltpu.SMEM)
     sem = pltpu.SemaphoreType
@@ -406,11 +397,11 @@
         pair_rep, residue_mask.reshape(1, -1), chain_index.reshape(1, -1), mul_in, mul_gate, mul_out, att_in, att_bias.T,
         chain_bias.reshape(1, -1), att_out, trans_up, trans_down,
     )
-    return pl.pallas_call(
+    parts = pl.pallas_call(
         kernel,
-        out_shape=jax.ShapeDtypeStruct(pair_rep.shape, BF16),
+        out_shape=jax.ShapeDtypeStruct((16, 8, 16, 128), BF16),
         in_specs=specs,
-        out_specs=vmem,
+        out_specs=pl.BlockSpec(memory_space=pl.ANY),
         scratch_shapes=[pltpu.VMEM(a.shape, a.dtype) for n, a in enumerate(args) if n != 8]
         + [
             pltpu.VMEM((2048, 128), F32),
@@ -442,7 +433,6 @@
             pltpu.VMEM((2, 512, 512), BF16),
             pltpu.VMEM((8, 256, 128), BF16),
             pltpu.VMEM((16, 8, 16, 128), BF16),
-            pltpu.VMEM((16, 8, 16, 128), BF16),
             sem.REGULAR((8,)),
             sem.DMA((11,)),
             sem.DMA((8,)),
@@ -453,6 +443,7 @@
         ],
         compiler_params=pltpu.CompilerParams(collective_id=0, has_side_effects=True, vmem_limit_bytes=56 * 1024 * 1024),
     )(*args)
+    return parts.reshape(8, 2, 8, 4, 4, 128).transpose(0, 2, 3, 1, 4, 5).reshape(pair_rep.shape)
 
 
 def solution(mesh):

time: 73 us -> 71.3 us (0.977)
  Pallas kernels: 70.9 us -> 69.1 us
    transpose x0 -> x1, local copies, waits for them, and re-layouts: none -> 2.03 us  [body(): parts.reshape(8, 2, 8, 4, 4, 128).transpose(0, 2, 3, 1, 4, 5)]
    unnamed x1 -> x0, local copies, waits for them, and re-layouts: 1.87 us -> none
    pallas_call x1, Pallas kernels: 70.9 us -> 69.1 us  [body(): pl.pallas_call(kernel, out_shape=jax.ShapeDtypeStruct((16, 8, 16, 128), B...]
where the time goes in v6:
time: 71.3 us; the launch traced here: 71.1 us
  Pallas kernels  69.1 us (97%)
  local copies, waits for them, and re-layouts  2.03 us (3%)
    pallas_call x1, Pallas kernels, body(): pl.pallas_call(kernel, out_shape=jax.ShapeDtypeStruct((16, 8, 16, 128), B...  69.1 us
    transpose x1, local copies, waits for them, and re-layouts, body(): parts.reshape(8, 2, 8, 4, 4, 128).transpose(0, 2, 3, 1, 4, 5)  2.03 us

profile of v6, /device:TPU:1, one launch (start us, length us, event | category | flops | bytes accessed | tf_op | source)
XLA Modules:
  0.0 71.1 jit_solution(214535004255518718)
XLA Ops:
  0.0 69.1 %shard_map.118 = bf16[16,8,16,128]{3,2,1,0:T(8,128)(2,1)} custom-call(bf16[64,32,128]{2,1,0:T(8,128)(2,1)} %pair_in.1, s32[1,512]{1,0:T(1,128)} %bitcast.9, s32[1,512]{1,0:T(1,128)} %bitcast.10, bf16[128,512]{1,0:T(8,128)(2,1)} %mul_in_in.1, bf16[128,128]{1,0:T(8,128)(2,1)} %mul_gate_in.1, bf16[128,128]{1,0:T(8,128)(2,1)} %mul_out_in.1, ...), custom_call_target="tpu_custom_call" | custom-call | tf_op jit(solution)/shard_map/pallas_call | solution.py:400
  69.1 2.0 %copy.13 = bf16[8,8,4,2,4,128]{5,4,3,2,1,0:T(4,128)(2,1)} copy(bf16[8,8,4,2,4,128]{5,4,2,1,3,0:T(4,128)(2,1)} %bitcast.8) | data formatting | bytes 1048576 | tf_op jit(solution)/shard_map/transpose | solution.py:446

commit v7 on v6

--- a/solution.py
+++ b/solution.py
@@ -213,7 +213,7 @@
                     ref, ref, gather_send.at[o, 0], gather_recv.at[o, 0], device_id=device_at(there), device_id_type=MESH
                 ).start()
             return carry
-        lax.fori_loop(1, 16, one, 0)
+        lax.fori_loop(1, 16, one, 0, unroll=True)
 
     def plane_wait(which):
         for o in which:
@@ -292,10 +292,10 @@
     for o in early:
         plane_wait((o,))
         axis_start((o,))
-    project(core * 4, normed_all[...].reshape(2048, 128))
     for o in late:
         plane_wait((o,))
         axis_start((o,))
+    project(core * 4, normed_all[...].reshape(2048, 128))
     swap.wait()
     other = 4 - core * 4
     project(other, norm(one_all[pl.ds(other, 4)].reshape(2048, 128).astype(F32), 1))
@@ -360,14 +360,14 @@
             c = lax.rem(col + s, 16)
             remote(out_s.at[c, rows], out_r.at[col, rows], 4 + part, (row, c)).start()
             return carry
-        lax.fori_loop(1, 16, one, 0)
+        lax.fori_loop(1, 16, one, 0, unroll=True)
         pltpu.make_async_copy(out_s.at[col, rows], out_r.at[col, rows], local.at[4 + part]).start()
 
     for i in range(8):
         score(0, i)
     for hp, group in enumerate((early, late)):
         axis_wait(group)
-        lax.fori_loop(0, 16, functools.partial(build, hp), 0)
+        lax.fori_loop(0, 16, functools.partial(build, hp), 0, unroll=4)
         for i in range(8):
             if hp == 0:
                 score(1, i)

time: 71.3 us -> 71.1 us (level)
  no operation moved by 1% of the time
where the time goes in v7:
time: 71.1 us; the launch traced here: 70.9 us
  Pallas kernels  68.9 us (97%)
  local copies, waits for them, and re-layouts  2.03 us (3%)
    pallas_call x1, Pallas kernels, body(): pl.pallas_call(kernel, out_shape=jax.ShapeDtypeStruct((16, 8, 16, 128), B...  68.9 us
    transpose x1, local copies, waits for them, and re-layouts, body(): parts.reshape(8, 2, 8, 4, 4, 128).transpose(0, 2, 3, 1, 4, 5)  2.03 us

profile of v7, /device:TPU:1, one launch (start us, length us, event | category | flops | bytes accessed | tf_op | source)
XLA Modules:
  0.0 70.9 jit_solution(11638125942280182481)
XLA Ops:
  0.0 68.9 %shard_map.118 = bf16[16,8,16,128]{3,2,1,0:T(8,128)(2,1)} custom-call(bf16[64,32,128]{2,1,0:T(8,128)(2,1)} %pair_in.1, s32[1,512]{1,0:T(1,128)} %bitcast.9, s32[1,512]{1,0:T(1,128)} %bitcast.10, bf16[128,512]{1,0:T(8,128)(2,1)} %mul_in_in.1, bf16[128,128]{1,0:T(8,128)(2,1)} %mul_gate_in.1, bf16[128,128]{1,0:T(8,128)(2,1)} %mul_out_in.1, ...), custom_call_target="tpu_custom_call" | custom-call | tf_op jit(solution)/shard_map/pallas_call | solution.py:400
  68.9 2.0 %copy.13 = bf16[8,8,4,2,4,128]{5,4,3,2,1,0:T(4,128)(2,1)} copy(bf16[8,8,4,2,4,128]{5,4,2,1,3,0:T(4,128)(2,1)} %bitcast.8) | data formatting | bytes 1048576 | tf_op jit(solution)/shard_map/transpose | solution.py:446

commit v8 on v7

--- a/solution.py
+++ b/solution.py
@@ -102,7 +102,7 @@
     pair_mask = jnp.where(lanes16 < 64, even, odd) * row_mask
     loads[1].wait()
     loads[2].wait()
-    pair_f[...] = pair_ref[...].astype(F32).reshape(2048, 128)
+    pair_f[0:2048] = pair_ref[...].astype(F32).reshape(2048, 128)
     mul_in_t = mul_in_ref[...].T
     for step in range(2):
         if step == 1:
@@ -119,7 +119,7 @@
         for v in range(8):
             lr_f[pl.ds(8 * step + v, 128, stride=32), :] = left[:, v * 128 : v * 128 + 128]
             lr_f[pl.ds(16 + 8 * step + v, 128, stride=32), :] = right[:, v * 128 : v * 128 + 128]
-    lr_s[...] = lr_f[...].reshape(128, 2, 16, 128).astype(BF16)
+    lr_s[...] = lr_f[0:4096].reshape(128, 2, 16, 128).astype(BF16)
 
     for one in loads[3:]:
         one.wait()
@@ -181,7 +181,7 @@
             at = rp * 128 + il * 32
             for jt in range(4):
                 m_f[pl.ds(rp * 512 + il * 4 + jt, 32, stride=16), :] = product[at : at + 32, jt * 128 : jt * 128 + 128]
-    m_s[...] = m_f[...].reshape(128, 16, 128).astype(BF16)
+    m_s[...] = m_f[0:2048].reshape(128, 16, 128).astype(BF16)
     to_all(m_s, m_r, 2)
 
     for part in range(2):
@@ -244,7 +244,7 @@
             whole.wait_send()
             whole.wait_recv()
 
-    m_f[...] = m_r[...].astype(F32).reshape(2048, 128)
+    m_f[0:2048] = m_r[...].astype(F32).reshape(2048, 128)
     bias_in = jnp.concatenate([att_bias_ref[...].astype(F32), jnp.zeros((4, 128), F32)], axis=0).astype(BF16)
     for half in range(2):
         tiles = [m_f[pl.ds(il * 4 + 2 * half + t, 128, stride=16), :] for il in range(4) for t in range(2)]
@@ -404,13 +404,13 @@
         out_specs=pl.BlockSpec(memory_space=pl.ANY),
         scratch_shapes=[pltpu.VMEM(a.shape, a.dtype) for n, a in enumerate(args) if n != 8]
         + [
-            pltpu.VMEM((2048, 128), F32),
-            pltpu.VMEM((4096, 128), F32),
+            pltpu.VMEM((2080, 128), F32),
+            pltpu.VMEM((4128, 128), F32),
             pltpu.VMEM((128, 2, 16, 128), BF16),
             pltpu.VMEM((128, 2, 16, 128), BF16),
             pltpu.VMEM((512, 512), BF16),
             pltpu.VMEM((512, 512), BF16),
-            pltpu.VMEM((2048, 128), F32),
+            pltpu.VMEM((2080, 128), F32),
             pltpu.VMEM((128, 16, 128), BF16),
             pltpu.VMEM((128, 16, 128), BF16),
             pltpu.VMEM((16, 4, 32, 128), BF16),

time: 71.1 us -> 71.1 us (level)
  no operation moved by 1% of the time
where the time goes in v8:
time: 71.1 us; the launch traced here: 70.9 us
  Pallas kernels  68.9 us (97%)
  local copies, waits for them, and re-layouts  2.03 us (3%)
    pallas_call x1, Pallas kernels, body(): pl.pallas_call(kernel, out_shape=jax.ShapeDtypeStruct((16, 8, 16, 128), B...  68.9 us
    transpose x1, local copies, waits for them, and re-layouts, body(): parts.reshape(8, 2, 8, 4, 4, 128).transpose(0, 2, 3, 1, 4, 5)  2.03 us

profile of v8, /device:TPU:1, one launch (start us, length us, event | category | flops | bytes accessed | tf_op | source)
XLA Modules:
  0.0 70.9 jit_solution(2990870835142087003)
XLA Ops:
  0.0 68.9 %shard_map.118 = bf16[16,8,16,128]{3,2,1,0:T(8,128)(2,1)} custom-call(bf16[64,32,128]{2,1,0:T(8,128)(2,1)} %pair_in.1, s32[1,512]{1,0:T(1,128)} %bitcast.9, s32[1,512]{1,0:T(1,128)} %bitcast.10, bf16[128,512]{1,0:T(8,128)(2,1)} %mul_in_in.1, bf16[128,128]{1,0:T(8,128)(2,1)} %mul_gate_in.1, bf16[128,128]{1,0:T(8,128)(2,1)} %mul_out_in.1, ...), custom_call_target="tpu_custom_call" | custom-call | tf_op jit(solution)/shard_map/pallas_call | solution.py:400
  68.9 2.0 %copy.13 = bf16[8,8,4,2,4,128]{5,4,3,2,1,0:T(4,128)(2,1)} copy(bf16[8,8,4,2,4,128]{5,4,2,1,3,0:T(4,128)(2,1)} %bitcast.8) | data formatting | bytes 1048576 | tf_op jit(solution)/shard_map/transpose | solution.py:446
